TPU v7x, 32 devices: a whole 2x2x4 slice. The times are simulated.
32 devices in a mesh: outer: 8 (over z, x), inner: 4 (over y, core).
Axes of the slice: x: 2, y: 2, z: 4, core: 2. Of those that a mesh axis runs over, the one named last changes fastest.
Arguments:
- activations: bfloat16 [8192, 8192], P(('outer', 'inner')), may hold values from -6 to 6
- output_grads: bfloat16 [8192, 512], P(('outer', 'inner')), may hold values from -0.06591797 to 0.06591797
- master_weights: float32 [8192, 512], P(('inner', 'outer')), may hold values from -0.0625 to 0.0625
- first_moment: float32 [8192, 512], P(('inner', 'outer')), may hold values from -5 to 5
- second_moment: float32 [8192, 512], P(('inner', 'outer')), may hold values from 0.1 to 2
- next_tokens: bfloat16 [8192, 8192], P(('outer', 'inner')), may hold values from -6 to 6
Outputs:
- new_master: float32 [8192, 512], P(('inner', 'outer'))
- new_first_moment: float32 [8192, 512], P(('inner', 'outer'))
- new_second_moment: float32 [8192, 512], P(('inner', 'outer'))
- kept_weights: bfloat16 [8192, 512], P('inner')
- projection: bfloat16 [8192, 512], P(('outer', 'inner'))
All inputs are finite; a program needn't handle non-finite values.
Results may differ from a plain program's by a relative error of at most 0.012.
Values may be sent and summed in bfloat16 or wider, within the bound.
A program may use at most 128 MiB of HBM per device.

v0:
```python
import jax
import jax.numpy as jnp
from jax import lax
from jax.sharding import PartitionSpec as P

ADAM_STEP = 10


beta_first = 0.9
beta_second = 0.95
learn_rate = 0.002
decay_rate = 0.1
adam_eps = 1e-08


def adamw_update(gradient, master_weights, first_moment, second_moment):
    new_first = beta_first * first_moment + (1.0 - beta_first) * gradient
    new_second = beta_second * second_moment + (1.0 - beta_second) * gradient * gradient
    first_hat = new_first / (1.0 - beta_first**ADAM_STEP)
    second_hat = new_second / (1.0 - beta_second**ADAM_STEP)
    new_master = master_weights - learn_rate * (
        first_hat / (jnp.sqrt(second_hat) + adam_eps) + decay_rate * master_weights
    )
    return (new_master, new_first, new_second)


def rounded_term(columns, output_grads):
    contrib = jnp.einsum(
        "tr,tc->rc", columns, output_grads, preferred_element_type=jnp.float32
    ).astype(jnp.bfloat16)
    contrib = lax.optimization_barrier(contrib)
    return contrib.astype(jnp.float32)


def regroup_features(activations, outer_count, inner_count):
    tok_rows, width = activations.shape
    shard_rows = width // (outer_count * inner_count)
    split_view = activations.reshape(tok_rows, inner_count, outer_count, shard_rows)
    return split_view.transpose(0, 2, 1, 3).reshape(tok_rows, width)


def local(activations, output_grads, master_weights, first_moment, second_moment, next_tokens):
    outer_count = lax.axis_size("outer")
    inner_count = lax.axis_size("inner")
    regrouped = regroup_features(activations, outer_count, inner_count)
    columns = regrouped
    gradient = lax.psum_scatter(
        rounded_term(columns, output_grads), ("outer", "inner"), scatter_dimension=0, tiled=True
    )
    new_master, new_first, new_second = adamw_update(
        gradient, master_weights, first_moment, second_moment
    )
    kept_shard = new_master.astype(jnp.bfloat16)
    kept_weights = lax.all_gather(kept_shard, "outer", axis=0, tiled=True)
    columns = next_tokens
    projected = jnp.dot(
        columns,
        lax.all_gather(kept_weights, "inner", axis=0, tiled=True),
        preferred_element_type=jnp.float32,
    )
    return (new_master, new_first, new_second, kept_weights, projected.astype(jnp.bfloat16))


def solution(mesh):
    placed = (
        P(("outer", "inner"), None),
        P(("outer", "inner"), None),
        P(("inner", "outer"), None),
        P(("inner", "outer"), None),
        P(("inner", "outer"), None),
        P(("outer", "inner"), None),
    )
    return jax.shard_map(
        local,
        mesh=mesh,
        in_specs=placed,
        out_specs=(
            P(("inner", "outer"), None),
            P(("inner", "outer"), None),
            P(("inner", "outer"), None),
            P("inner", None),
            P(("outer", "inner"), None),
        ),
        check_vma=False,
    )
```

profile of v0, /device:TPU:1, one launch (start us, length us, event | category | flops | bytes accessed | tf_op | source)
XLA Modules:
  0.0 346.5 jit_solution(12504769043411838449)
XLA Ops:
  7.2 0.0 copy-start
  7.2 0.0 reduce-scatter.2.cloned.1.call-start
  7.2 6.4 %copy.13 = bf16[256,8192]{0,1:T(8,128)(2,1)} copy(bf16[256,8192]{1,0:T(8,128)(2,1)} %param.6) | data formatting | bytes 8388608 | tf_op args[0]
  13.6 2.5 copy.14
  16.1 0.0 copy-done
  16.1 5.6 %convolution_convert_fusion = bf16[8192,512]{1,0:T(8,128)(2,1)} fusion(bf16[256,8192]{0,1:T(8,128)(2,1)S(1)} %bitcast.10, bf16[256,512]{1,0:T(8,128)(2,1)S(1)} %copy-done), kind=kOutput, calls=%fused_computation | convolution fusion | flops 2151677952 | bytes 12845056 | tf_op jit(solution)/shard_map/tr,tc->rc/dot_general | solution.py:28
  21.7 11.5 %convert_element_type.16 = f32[8192,512]{1,0:T(8,128)} convert(bf16[8192,512]{1,0:T(8,128)(2,1)} %convolution_convert_fusion) | non-fusion elementwise | flops 4194304 | bytes 25165824 | tf_op jit(solution)/shard_map/convert_element_type | solution.py:32
  33.2 0.0 copy-start.2
  33.2 0.0 copy-start.3
  33.2 0.0 copy-start.4
  33.2 0.0 reduce-scatter.2.cloned.1.call-update
  33.2 0.0 all-gather.3.cloned.1.call-start
  33.3 186.1 %reduce-scatter.2.cloned.1.call-done = f32[256,512]{1,0:T(8,128)} async-done(((f32[8192,512]{1,0:T(8,128)}), f32[256,512]{1,0:T(8,128)}) %reduce-scatter.2.cloned.1.call-update) | async-done | bytes 524304 | tf_op jit(solution)/shard_map/reduce_scatter | solution.py:47
  219.4 0.0 copy-done.2
  219.4 0.0 copy-done.3
  219.4 0.0 copy-done.4
  219.4 2.5 fusion.2
  221.9 0.0 all-gather.3.cloned.1.call-update
  222.0 0.0 all-gather.5.cloned.1.call-start
  222.0 49.0 %all-gather.3.cloned.1.call-done = bf16[2048,512]{1,0:T(8,128)(2,1)} async-done(((bf16[256,512]{1,0:T(8,128)(2,1)}), bf16[2048,512]{1,0:T(8,128)(2,1)}) %all-gather.3.cloned.1.call-update) | async-done | bytes 2097168 | tf_op jit(solution)/shard_map/all_gather | solution.py:54
  271.0 0.0 all-gather.5.cloned.1.call-update
  271.0 0.0 copy-start.1
  271.0 59.9 %all-gather.5.cloned.1.call-done = bf16[8192,512]{1,0:T(8,128)(2,1)} async-done(((bf16[2048,512]{1,0:T(8,128)(2,1)}), bf16[8192,512]{1,0:T(8,128)(2,1)}) %all-gather.5.cloned.1.call-update) | async-done | bytes 8388624 | tf_op jit(solution)/shard_map/all_gather | solution.py:58
  330.9 6.9 %fusion = bf16[256,512]{0,1:T(8,128)(2,1)S(1)} fusion(bf16[8192,512]{1,0:T(8,128)(2,1)} %all-gather.5.cloned.1.call-done, bf16[256,8192]{1,0:T(8,128)(2,1)} %param.11), kind=kOutput, calls=%fused_computation.2 | convolution fusion | flops 2147614720 | bytes 12845056 | tf_op jit(solution)/shard_map/dot_general | solution.py:56
  337.8 0.8 copy.15
  338.7 0.0 copy-done.1
  338.7 1.3 copy.17
Async XLA Ops:
  7.2 8.9 %copy-start = (bf16[256,512]{1,0:T(8,128)(2,1)S(1)}, bf16[256,512]{1,0:T(8,128)(2,1)}, u32[]{:S(2)}) copy-start(bf16[256,512]{1,0:T(8,128)(2,1)} %param.7) | copy-start | bytes 786436
  7.2 212.2 %reduce-scatter.2.cloned.1.call-start = ((), (), s32[]{:S(2)}) async-start(), calls=%async_computation.1 | async-start | bytes 17301504 | tf_op jit(solution)/shard_map/reduce_scatter | solution.py:47
  33.2 186.2 %copy-start.2 = (f32[256,512]{1,0:T(8,128)S(1)}, f32[256,512]{1,0:T(8,128)}, u32[]{:S(2)}) copy-start(f32[256,512]{1,0:T(8,128)} %param.8) | copy-start | bytes 1572868
  33.2 186.2 %copy-start.3 = (f32[256,512]{1,0:T(8,128)S(1)}, f32[256,512]{1,0:T(8,128)}, u32[]{:S(2)}) copy-start(f32[256,512]{1,0:T(8,128)} %param.9) | copy-start | bytes 1572868
  33.2 186.2 %copy-start.4 = (f32[256,512]{1,0:T(8,128)S(1)}, f32[256,512]{1,0:T(8,128)}, u32[]{:S(2)}) copy-start(f32[256,512]{1,0:T(8,128)} %param.10) | copy-start | bytes 1572868
  33.2 237.7 %all-gather.3.cloned.1.call-start = ((), (), s32[]{:S(2)}) async-start(), calls=%async_computation.2 | async-start | bytes 2359296 | tf_op jit(solution)/shard_map/all_gather | solution.py:54
  222.0 108.9 %all-gather.5.cloned.1.call-start = ((), (), s32[]{:S(2)}) async-start(), calls=%async_computation.3 | async-start | bytes 10485760 | tf_op jit(solution)/shard_map/all_gather | solution.py:58
  271.0 67.7 %copy-start.1 = (bf16[2048,512]{1,0:T(8,128)(2,1)S(1)}, bf16[2048,512]{1,0:T(8,128)(2,1)}, u32[]{:S(2)}) copy-start(bf16[2048,512]{1,0:T(8,128)(2,1)} %all-gather.3.cloned.1.call-done) | copy-start | bytes 6291460
Sparse Core Ops, SparseCore 0:
  33.4 185.9 reduce-scatter.1
  222.1 48.8 all-gather.2
  272.5 58.3 all-gather.4
where the time goes:
time: 347 us
  waiting for transfers between devices  295 us (85%)
  other arithmetic  14.1 us (4%)
  between operations  13.8 us (4%)
  matrix products  12.5 us (4%)
  local copies, waits for them, and re-layouts  11.1 us (3%)
    reduce_scatter x1, waiting for transfers between devices, local(): lax.psum_scatter(rounded_term(columns, output_grads), ('outer', 'inner'),...  186 us
    all_gather x1, waiting for transfers between devices, local(): lax.all_gather(kept_weights, 'inner', axis=0, tiled=True)  59.9 us
    all_gather x1, waiting for transfers between devices, local(): kept_weights = lax.all_gather(kept_shard, 'outer', axis=0, tiled=True)  49 us
    convert_element_type x1, other arithmetic, rounded_term(): return contrib.astype(jnp.float32)  11.5 us
    unnamed x13, local copies, waits for them, and re-layouts  8.61 us
  transfers between devices with their start and end apart: 3, of which 3 were waited for; matrix products, arithmetic and copies ran while one was open for 0% of the time, Pallas kernels for 0%

commit v1 on v0

--- a/solution.py
+++ b/solution.py
@@ -1,9 +1,16 @@
+import functools
+
 import jax
 import jax.numpy as jnp
 from jax import lax
+from jax.experimental import pallas as pl
+from jax.experimental.pallas import tpu as pltpu
 from jax.sharding import PartitionSpec as P
 
 ADAM_STEP = 10
+MESH = pl.DeviceIdType.MESH
+BF16 = jnp.bfloat16
+F32 = jnp.float32
 
 
 beta_first = 0.9
@@ -39,26 +46,347 @@
     return split_view.transpose(0, 2, 1, 3).reshape(tok_rows, width)
 
 
-def local(activations, output_grads, master_weights, first_moment, second_moment, next_tokens):
+def local_plain(activations, output_grads, master_weights, first_moment, second_moment, next_tokens):
     outer_count = lax.axis_size("outer")
     inner_count = lax.axis_size("inner")
     regrouped = regroup_features(activations, outer_count, inner_count)
-    columns = regrouped
     gradient = lax.psum_scatter(
-        rounded_term(columns, output_grads), ("outer", "inner"), scatter_dimension=0, tiled=True
+        rounded_term(regrouped, output_grads), ("outer", "inner"), scatter_dimension=0, tiled=True
     )
     new_master, new_first, new_second = adamw_update(
         gradient, master_weights, first_moment, second_moment
     )
     kept_shard = new_master.astype(jnp.bfloat16)
     kept_weights = lax.all_gather(kept_shard, "outer", axis=0, tiled=True)
-    columns = next_tokens
     projected = jnp.dot(
-        columns,
+        next_tokens,
         lax.all_gather(kept_weights, "inner", axis=0, tiled=True),
         preferred_element_type=jnp.float32,
     )
     return (new_master, new_first, new_second, kept_weights, projected.astype(jnp.bfloat16))
+
+
+class Plan:
+    def __init__(self, n_out, n_in, rows, cols):
+        self.n_out, self.n_in, self.rows, self.cols = n_out, n_in, rows, cols
+        out_bits = [("outer", k) for k in range(n_out.bit_length() - 1)]
+        in_bits = [("inner", k) for k in range(1, n_in.bit_length() - 1)]
+        ranked = []
+        for k in range(max(len(out_bits), len(in_bits))):
+            ranked += out_bits[k : k + 1] + in_bits[k : k + 1]
+        self.dims = ranked[::-1]
+        self.depth = len(ranked)
+        self.blocks = 2**self.depth
+        top = self.depth - 1
+        first = tuple(range(top, -1, -1))
+        second = (top - 1, top) + first[2:]
+        self.parts = [
+            (first, (0, cols // 2), (0, rows // 2)),
+            (second, (cols // 2, cols // 2), (rows // 2, rows // 2)),
+        ]
+
+    def canon(self, p, k):
+        order = self.parts[p][0]
+        return sum(((k >> t) & 1) << order[self.depth - 1 - t] for t in range(self.depth))
+
+
+def kernel(plan, *refs):
+    (act_h, grad_h, mw_h, m1_h, m2_h, nt_h, nm_o, n1_o, n2_o, kept_o, proj_o) = refs[:11]
+    (act, grad, nt, mw, m1, m2, nm, n1, n2, grad_t, own, snd0, rcv0, total, weights, acc) = refs[11:27]
+    n_parts, depth, blocks = len(plan.parts), plan.depth, plan.blocks
+    rv_flat = refs[27 : 27 + n_parts * depth]
+    (core_send, core_recv, rs_send, rs_recv, ag_send, ag_recv, cg_send, cg_recv, local) = refs[
+        27 + n_parts * depth :
+    ]
+    rv = [rv_flat[p * depth : (p + 1) * depth] for p in range(n_parts)]
+    R, C = plan.rows, plan.cols
+
+    loads = [
+        pltpu.make_async_copy(s, d, local.at[i])
+        for i, (s, d) in enumerate(
+            [(grad_h, grad), (act_h, act), (mw_h, mw), (m1_h, m1), (m2_h, m2), (nt_h, nt)]
+        )
+    ]
+    for load in loads:
+        load.start()
+
+    outer, inner = lax.axis_index("outer"), lax.axis_index("inner")
+    place = {"outer": outer, "inner": inner}
+
+    def bit(axis, k):
+        return (place[axis] // 2**k) % 2
+
+    def partner(axis, k):
+        other = place[axis] + (1 - 2 * bit(axis, k)) * 2**k
+        return (other, inner) if axis == "outer" else (outer, other)
+
+    sibling = partner("inner", 0)
+    others = [partner(axis, k) for axis, k in plan.dims]
+
+    barrier = pltpu.get_barrier_semaphore()
+    for device in [sibling] + others:
+        pl.semaphore_signal(barrier, inc=1, device_id=device, device_id_type=MESH)
+
+    def block_at(flip_core, c):
+        o, n = outer, inner
+        if flip_core:
+            n = n + 1 - 2 * bit("inner", 0)
+        for j, (axis, k) in enumerate(plan.dims):
+            step = ((c // 2**j) % 2) * (1 - 2 * bit(axis, k)) * 2**k
+            if axis == "outer":
+                o = o + step
+            else:
+                n = n + step
+        return o, n
+
+    def columns(flip_core, c):
+        o, n = block_at(flip_core, c)
+        return pl.ds(pl.multiple_of((n * plan.n_out + o) * R, R), R)
+
+    loads[0].wait()
+    grad_t[...] = grad[...].astype(F32).T.astype(BF16)
+    loads[1].wait()
+    pl.semaphore_wait(barrier, 1 + depth)
+
+    def core_copy(c):
+        return pltpu.make_async_remote_copy(
+            src_ref=snd0.at[c],
+            dst_ref=rcv0.at[c],
+            send_sem=core_send.at[c],
+            recv_sem=core_recv.at[c],
+            device_id=sibling,
+            device_id_type=MESH,
+        )
+
+    @pl.loop(0, blocks)
+    def _(i):
+        c = blocks - 1 - i
+        snd0[c] = jnp.dot(
+            grad_t[...], act[:, columns(True, c)], preferred_element_type=F32
+        ).astype(BF16)
+        core_copy(c).start()
+
+    @pl.loop(0, blocks)
+    def _(i):
+        c = blocks - 1 - i
+        own[c] = jnp.dot(
+            grad_t[...], act[:, columns(False, c)], preferred_element_type=F32
+        ).astype(BF16)
+
+    sums = {}
+    arrived = set()
+
+    def need(key, copy):
+        if key not in arrived:
+            arrived.add(key)
+            copy.wait_recv()
+
+    tile = 64
+
+    def gather_terms(p, k, steps, dst, dst_dtype):
+        _, (lo, count), _ = plan.parts[p]
+        c = plan.canon(p, k)
+        need(("core", c), core_copy(c))
+        for t in range(steps):
+            need((p, t, k), sums[(p, k + 2 ** (depth - 1 - t))])
+
+        @pl.loop(0, count // tile)
+        def _(i):
+            at = pl.multiple_of(i * tile, tile)
+            span = pl.ds(lo + at, tile)
+            value = own[c, span, :].astype(F32) + rcv0[c, span, :].astype(F32)
+            for t in range(steps):
+                value += rv[p][t][k, pl.ds(at, tile), :].astype(F32)
+            if dst is None:
+                own[c, span, :] = value.astype(dst_dtype)
+            else:
+                dst[span, :] = value
+
+    for k in range(blocks - 1, 0, -1):
+        for p in range(n_parts):
+            order, (lo, count), _ = plan.parts[p]
+            high = k.bit_length() - 1
+            step = depth - 1 - high
+            gather_terms(p, k, step, None, BF16)
+            c = plan.canon(p, k)
+            copy = pltpu.make_async_remote_copy(
+                src_ref=own.at[c, pl.ds(lo, count)],
+                dst_ref=rv[p][step].at[k - 2**high],
+                send_sem=rs_send.at[p, k],
+                recv_sem=rs_recv.at[p, k],
+                device_id=others[order[step]],
+                device_id_type=MESH,
+            )
+            copy.start()
+            sums[(p, k)] = copy
+    for p in range(n_parts):
+        gather_terms(p, 0, depth, total, F32)
+
+    for load in loads[2:5]:
+        load.wait()
+    half = R // n_parts
+    for p in range(n_parts):
+        lo = p * half
+        gradient = total[:, lo : lo + half].T
+        span = pl.ds(lo, half)
+        master, first, second = adamw_update(gradient, mw[span, :], m1[span, :], m2[span, :])
+        nm[span, :] = master
+        n1[span, :] = first
+        n2[span, :] = second
+        weights[0, 0, span, :] = master.astype(BF16)
+
+    stores = [
+        pltpu.make_async_copy(s, d, local.at[6 + i])
+        for i, (s, d) in enumerate([(nm, nm_o), (n1, n1_o), (n2, n2_o)])
+    ]
+    for store in stores:
+        store.start()
+
+    acc[...] = jnp.zeros_like(acc)
+    loads[5].wait()
+
+    def project(side, c):
+        acc[...] += jnp.dot(
+            nt[:, columns(side == 1, c)], weights[side, c], preferred_element_type=F32
+        )
+
+    passed, crossed, keeps = {}, {}, []
+    have = {c: 0 for c in range(blocks)}
+    inner_mask = sum(2**j for j, (axis, _) in enumerate(plan.dims) if axis == "inner")
+    pending = []
+
+    def finish_sibling(c):
+        for p in range(n_parts):
+            crossed[(p, c)].wait_recv()
+        project(1, c)
+
+    for q in range(blocks):
+        ready = []
+        for p in range(n_parts):
+            order, _, (lo, count) = plan.parts[p]
+            c = plan.canon(p, q)
+            high = q.bit_length() - 1
+            if q > 0:
+                passed[(p, q - 2**high, high)].wait_recv()
+            rows = pl.ds(lo, count)
+            for t in range(high + 1, depth):
+                e = order[depth - 1 - t]
+                copy = pltpu.make_async_remote_copy(
+                    src_ref=weights.at[0, c, rows],
+                    dst_ref=weights.at[0, c + 2**e, rows],
+                    send_sem=ag_send.at[p, q + 2**t],
+                    recv_sem=ag_recv.at[p, q + 2**t],
+                    device_id=others[e],
+                    device_id_type=MESH,
+                )
+                copy.start()
+                passed[(p, q, t)] = copy
+            copy = pltpu.make_async_remote_copy(
+                src_ref=weights.at[0, c, rows],
+                dst_ref=weights.at[1, c, rows],
+                send_sem=cg_send.at[p, c],
+                recv_sem=cg_recv.at[p, c],
+                device_id=sibling,
+                device_id_type=MESH,
+            )
+            copy.start()
+            crossed[(p, c)] = copy
+            have[c] += 1
+            if have[c] == n_parts:
+                ready.append(c)
+        for c in ready:
+            if c & inner_mask == 0:
+                o, _ = block_at(False, c)
+                keep = pltpu.make_async_copy(
+                    weights.at[0, c],
+                    kept_o.at[pl.ds(pl.multiple_of(o * R, R), R)],
+                    local.at[9 + len(keeps)],
+                )
+                keep.start()
+                keeps.append(keep)
+            project(0, c)
+            pending.append(c)
+        while len(pending) > 2:
+            finish_sibling(pending.pop(0))
+    for c in pending:
+        finish_sibling(c)
+    proj_o[...] = acc[...].astype(BF16)
+
+    for c in range(blocks):
+        core_copy(c).wait_send()
+    for copy in list(sums.values()) + list(passed.values()) + list(crossed.values()):
+        copy.wait_send()
+    for copy in stores + keeps:
+        copy.wait()
+
+
+def local_kernel(activations, output_grads, master_weights, first_moment, second_moment, next_tokens):
+    n_out, n_in = lax.axis_size("outer"), lax.axis_size("inner")
+    tokens, width = activations.shape
+    next_rows = next_tokens.shape[0]
+    R, C = master_weights.shape
+    plan = Plan(n_out, n_in, R, C)
+    B, L, n_parts = plan.blocks, plan.depth, len(plan.parts)
+    dma = pltpu.SemaphoreType.DMA
+    any_spec = pl.BlockSpec(memory_space=pl.ANY)
+    arrived = [
+        pltpu.VMEM((2 ** (L - 1 - s), count, R), BF16)
+        for _, (_, count), _ in plan.parts
+        for s in range(L)
+    ]
+    return pl.pallas_call(
+        functools.partial(kernel, plan),
+        out_shape=(
+            jax.ShapeDtypeStruct((R, C), F32),
+            jax.ShapeDtypeStruct((R, C), F32),
+            jax.ShapeDtypeStruct((R, C), F32),
+            jax.ShapeDtypeStruct((n_out * R, C), BF16),
+            jax.ShapeDtypeStruct((next_rows, C), BF16),
+        ),
+        in_specs=[any_spec] * 6,
+        out_specs=(any_spec,) * 4 + (pl.BlockSpec(memory_space=pltpu.VMEM),),
+        scratch_shapes=[
+            pltpu.VMEM((tokens, width), BF16),
+            pltpu.VMEM((tokens, C), BF16),
+            pltpu.VMEM((next_rows, width), BF16),
+        ]
+        + [pltpu.VMEM((R, C), F32)] * 6
+        + [
+            pltpu.VMEM((C, tokens), BF16),
+            pltpu.VMEM((B, C, R), BF16),
+            pltpu.VMEM((B, C, R), BF16),
+            pltpu.VMEM((B, C, R), BF16),
+            pltpu.VMEM((C, R), F32),
+            pltpu.VMEM((2, B, R, C), BF16),
+            pltpu.VMEM((next_rows, C), F32),
+        ]
+        + arrived
+        + [
+            dma((B,)),
+            dma((B,)),
+            dma((n_parts, B)),
+            dma((n_parts, B)),
+            dma((n_parts, B)),
+            dma((n_parts, B)),
+            dma((n_parts, B)),
+            dma((n_parts, B)),
+            dma((9 + n_out,)),
+        ],
+        compiler_params=pltpu.CompilerParams(
+            collective_id=0, has_side_effects=True, vmem_limit_bytes=58 * 2**20
+        ),
+        cost_estimate=pl.CostEstimate(
+            flops=2 * (tokens + next_rows) * width * C,
+            bytes_accessed=2 * (tokens + next_rows) * width + 24 * R * C,
+            transcendentals=R * C,
+        ),
+    )(activations, output_grads, master_weights, first_moment, second_moment, next_tokens)
+
+
+def fits_kernel(mesh):
+    n_out, n_in = mesh.shape["outer"], mesh.shape["inner"]
+    powers = n_out & (n_out - 1) == 0 and n_in & (n_in - 1) == 0
+    return powers and n_out >= 2 and n_in >= 4 and n_out * n_in <= 32
 
 
 def solution(mesh):
@@ -71,7 +399,7 @@
         P(("outer", "inner"), None),
     )
     return jax.shard_map(
-        local,
+        local_kernel if fits_kernel(mesh) else local_plain,
         mesh=mesh,
         in_specs=placed,
         out_specs=(

time: 347 us -> 111 us (0.32)
  waiting for transfers between devices: 295 us -> 0 us
  Pallas kernels: 0 us -> 102 us
  other arithmetic: 14.1 us -> 0 us
  between operations: 13.8 us -> 0.66 us
  matrix products: 12.5 us -> 0 us
    reduce_scatter x1 -> x0, waiting for transfers between devices: 186 us -> none  [local(): lax.psum_scatter(rounded_term(columns, output_grads), ('outer', 'inner'),...]
    all_gather x2 -> x0, waiting for transfers between devices: 109 us -> none  [the longest x1 59.9 us: local(): lax.all_gather(kept_weights, 'inner', axis=0, tiled=True)]
    pallas_call x0 -> x1, Pallas kernels: none -> 102 us  [local_kernel(): pl.pallas_call(functools.partial(kernel, plan), out_shape=(jax.ShapeDtype...]
    convert_element_type x2 -> x0, other arithmetic: 14.1 us -> none  [the longest x1 11.5 us: rounded_term(): return contrib.astype(jnp.float32)]
    dot_general x2 -> x0, matrix products: 12.5 us -> none  [the longest x1 6.94 us: local(): jnp.dot(columns, lax.all_gather(kept_weights, 'inner', axis=0, tiled=True...]
    unnamed x13 -> x9, local copies, waits for them, and re-layouts: 8.61 us -> 7.78 us
  transfers between devices with their start and end apart: 3 -> 0, of which waited for: 3 -> 0; matrix products, arithmetic and copies ran while one was open for 0% -> 0% of each run, Pallas kernels for 0% -> 0%
where the time goes in v1:
time: 111 us; the launch traced here: 110 us
  Pallas kernels  102 us (92%)
  local copies, waits for them, and re-layouts  7.78 us (7%)
    pallas_call x1, Pallas kernels, local_kernel(): pl.pallas_call(functools.partial(kernel, plan), out_shape=(jax.ShapeDtype...  102 us
    unnamed x9, local copies, waits for them, and re-layouts  7.78 us

profile of v1, /device:TPU:1, one launch (start us, length us, event | category | flops | bytes accessed | tf_op | source)
XLA Modules:
  0.0 110.5 jit_solution(14774650717236298210)
XLA Ops:
  0.6 102.0 %shard_map.101 = (f32[256,512]{1,0:T(8,128)}, f32[256,512]{1,0:T(8,128)}, f32[256,512]{1,0:T(8,128)}, bf16[2048,512]{1,0:T(8,128)(2,1)}, bf16[256,512]{1,0:T(8,128)(2,1)}) custom-call(bf16[256,8192]{1,0:T(8,128)(2,1)} %refs_0_.1, bf16[256,512]{1,0:T(8,128)(2,1)} %refs_1_.1, f32[256,512]{1,0:T(8,128)} %refs_2_.1, f32[256,512]{1,0:T(8,128)} %refs_3_.1, ...), custom_call_target="tpu_custom_call" | custom-call | flops 4294967296 | bytes 11534336 | tf_op jit(solution)/shard_map/pallas_call | solution.py:337
  102.7 0.0 copy-start
  102.7 0.0 copy-start.1
  102.7 2.0 %copy.16 = f32[256,512]{1,0:T(8,128)} copy(f32[256,512]{1,0:T(8,128)} %get-tuple-element.10) | data formatting | bytes 1048576
  104.7 1.9 %copy.17 = f32[256,512]{1,0:T(8,128)} copy(f32[256,512]{1,0:T(8,128)} %get-tuple-element.11) | data formatting | bytes 1048576
  106.6 1.9 %copy.18 = f32[256,512]{1,0:T(8,128)} copy(f32[256,512]{1,0:T(8,128)} %get-tuple-element.12) | data formatting | bytes 1048576
  108.4 0.0 copy-done
  108.4 1.3 %copy.19 = bf16[2048,512]{1,0:T(8,128)(2,1)} copy(bf16[2048,512]{1,0:T(8,128)(2,1)S(1)} %copy-done) | data formatting | bytes 4194304
  109.8 0.0 copy-done.1
  109.8 0.7 copy.20
Async XLA Ops:
  102.7 5.8 %copy-start = (bf16[2048,512]{1,0:T(8,128)(2,1)S(1)}, bf16[2048,512]{1,0:T(8,128)(2,1)}, u32[]{:S(2)}) copy-start(bf16[2048,512]{1,0:T(8,128)(2,1)} %get-tuple-element.13) | copy-start | bytes 6291460
  102.7 7.1 %copy-start.1 = (bf16[256,512]{1,0:T(8,128)(2,1)S(1)}, bf16[256,512]{1,0:T(8,128)(2,1)}, u32[]{:S(2)}) copy-start(bf16[256,512]{1,0:T(8,128)(2,1)} %get-tuple-element.14) | copy-start | bytes 786436

commit v2 on v1

--- a/solution.py
+++ b/solution.py
@@ -64,6 +64,10 @@
         preferred_element_type=jnp.float32,
     )
     return (new_master, new_first, new_second, kept_weights, projected.astype(jnp.bfloat16))
+
+
+SUM_ORDERS = [((3, 0, 2, 1), 1), ((2, 1, 3, 0), 1)]
+GATHER_ORDERS = [((3, 1, 2, 0), 1), ((2, 0, 3, 1), 1)]
 
 
 class Plan:
@@ -77,38 +81,43 @@
         self.dims = ranked[::-1]
         self.depth = len(ranked)
         self.blocks = 2**self.depth
-        top = self.depth - 1
-        first = tuple(range(top, -1, -1))
-        second = (top - 1, top) + first[2:]
-        self.parts = [
-            (first, (0, cols // 2), (0, rows // 2)),
-            (second, (cols // 2, cols // 2), (rows // 2, rows // 2)),
-        ]
-
-    def canon(self, p, k):
-        order = self.parts[p][0]
+        self.sum_parts = self.cut(cols, SUM_ORDERS)
+        self.keep_parts = self.cut(rows, GATHER_ORDERS)
+
+    def cut(self, extent, orders):
+        plain = tuple(range(self.depth - 1, -1, -1))
+        share = sum(weight for _, weight in orders)
+        parts, lo = [], 0
+        for order, weight in orders:
+            count = extent * weight // share
+            parts.append((order if self.depth == len(order) else plain, lo, count))
+            lo += count
+        return parts
+
+    def canon(self, order, k):
         return sum(((k >> t) & 1) << order[self.depth - 1 - t] for t in range(self.depth))
 
 
 def kernel(plan, *refs):
     (act_h, grad_h, mw_h, m1_h, m2_h, nt_h, nm_o, n1_o, n2_o, kept_o, proj_o) = refs[:11]
     (act, grad, nt, mw, m1, m2, nm, n1, n2, grad_t, own, snd0, rcv0, total, weights, acc) = refs[11:27]
-    n_parts, depth, blocks = len(plan.parts), plan.depth, plan.blocks
-    rv_flat = refs[27 : 27 + n_parts * depth]
-    (core_send, core_recv, rs_send, rs_recv, ag_send, ag_recv, cg_send, cg_recv, local) = refs[
-        27 + n_parts * depth :
-    ]
-    rv = [rv_flat[p * depth : (p + 1) * depth] for p in range(n_parts)]
+    depth, blocks = plan.depth, plan.blocks
+    sum_parts, keep_parts = plan.sum_parts, plan.keep_parts
+    rv_flat = refs[27 : 27 + len(sum_parts) * depth]
+    (
+        load_sem,
+        core_send,
+        core_recv,
+        rs_send,
+        rs_recv,
+        ag_send,
+        ag_recv,
+        cg_send,
+        cg_recv,
+        local,
+    ) = refs[27 + len(sum_parts) * depth :]
+    rv = [rv_flat[p * depth : (p + 1) * depth] for p in range(len(sum_parts))]
     R, C = plan.rows, plan.cols
-
-    loads = [
-        pltpu.make_async_copy(s, d, local.at[i])
-        for i, (s, d) in enumerate(
-            [(grad_h, grad), (act_h, act), (mw_h, mw), (m1_h, m1), (m2_h, m2), (nt_h, nt)]
-        )
-    ]
-    for load in loads:
-        load.start()
 
     outer, inner = lax.axis_index("outer"), lax.axis_index("inner")
     place = {"outer": outer, "inner": inner}
@@ -143,13 +152,43 @@
         o, n = block_at(flip_core, c)
         return pl.ds(pl.multiple_of((n * plan.n_out + o) * R, R), R)
 
-    loads[0].wait()
+    sequence = []
+    for k in range(blocks - 1, -1, -1):
+        for order, _, _ in sum_parts:
+            c = plan.canon(order, k)
+            if k >= blocks // 2 and c not in sequence:
+                sequence.append(c)
+    sequence += [c for c in range(blocks - 1, -1, -1) if c not in sequence]
+
+    first_load = pltpu.make_async_copy(grad_h, grad, local.at[0])
+    first_load.start()
+    act_loads = {}
+    for c in sequence:
+        for side in (1, 0):
+            load = pltpu.make_async_copy(
+                act_h.at[:, columns(side == 1, c)], act.at[side, c], load_sem.at[side, c]
+            )
+            load.start()
+            act_loads[(side, c)] = load
+    loads = [
+        pltpu.make_async_copy(s, d, local.at[1 + i])
+        for i, (s, d) in enumerate([(mw_h, mw), (m1_h, m1), (m2_h, m2), (nt_h, nt)])
+    ]
+    for load in loads:
+        load.start()
+
+    first_load.wait()
     grad_t[...] = grad[...].astype(F32).T.astype(BF16)
-    loads[1].wait()
-    pl.semaphore_wait(barrier, 1 + depth)
-
-    def core_copy(c):
-        return pltpu.make_async_remote_copy(
+
+    cores = {}
+
+    def term(side, c):
+        act_loads[(side, c)].wait()
+        return jnp.dot(grad_t[...], act[side, c], preferred_element_type=F32).astype(BF16)
+
+    def send_term(c):
+        snd0[c] = term(1, c)
+        copy = pltpu.make_async_remote_copy(
             src_ref=snd0.at[c],
             dst_ref=rcv0.at[c],
             send_sem=core_send.at[c],
@@ -157,38 +196,21 @@
             device_id=sibling,
             device_id_type=MESH,
         )
-
-    @pl.loop(0, blocks)
-    def _(i):
-        c = blocks - 1 - i
-        snd0[c] = jnp.dot(
-            grad_t[...], act[:, columns(True, c)], preferred_element_type=F32
-        ).astype(BF16)
-        core_copy(c).start()
-
-    @pl.loop(0, blocks)
-    def _(i):
-        c = blocks - 1 - i
-        own[c] = jnp.dot(
-            grad_t[...], act[:, columns(False, c)], preferred_element_type=F32
-        ).astype(BF16)
+        copy.start()
+        cores[c] = copy
 
     sums = {}
     arrived = set()
-
-    def need(key, copy):
-        if key not in arrived:
-            arrived.add(key)
-            copy.wait_recv()
-
     tile = 64
 
-    def gather_terms(p, k, steps, dst, dst_dtype):
-        _, (lo, count), _ = plan.parts[p]
-        c = plan.canon(p, k)
-        need(("core", c), core_copy(c))
+    def gather_terms(p, k, steps, dst):
+        order, lo, count = sum_parts[p]
+        c = plan.canon(order, k)
+        if c not in arrived:
+            arrived.add(c)
+            cores[c].wait_recv()
         for t in range(steps):
-            need((p, t, k), sums[(p, k + 2 ** (depth - 1 - t))])
+            sums[(p, k + 2 ** (depth - 1 - t))].wait_recv()
 
         @pl.loop(0, count // tile)
         def _(i):
@@ -198,52 +220,55 @@
             for t in range(steps):
                 value += rv[p][t][k, pl.ds(at, tile), :].astype(F32)
             if dst is None:
-                own[c, span, :] = value.astype(dst_dtype)
+                own[c, span, :] = value.astype(BF16)
             else:
                 dst[span, :] = value
 
-    for k in range(blocks - 1, 0, -1):
-        for p in range(n_parts):
-            order, (lo, count), _ = plan.parts[p]
-            high = k.bit_length() - 1
-            step = depth - 1 - high
-            gather_terms(p, k, step, None, BF16)
-            c = plan.canon(p, k)
-            copy = pltpu.make_async_remote_copy(
-                src_ref=own.at[c, pl.ds(lo, count)],
-                dst_ref=rv[p][step].at[k - 2**high],
-                send_sem=rs_send.at[p, k],
-                recv_sem=rs_recv.at[p, k],
-                device_id=others[order[step]],
-                device_id_type=MESH,
-            )
-            copy.start()
-            sums[(p, k)] = copy
-    for p in range(n_parts):
-        gather_terms(p, 0, depth, total, F32)
-
-    for load in loads[2:5]:
-        load.wait()
-    half = R // n_parts
-    for p in range(n_parts):
-        lo = p * half
-        gradient = total[:, lo : lo + half].T
-        span = pl.ds(lo, half)
+    def send_sum(p, k):
+        order, lo, count = sum_parts[p]
+        high = k.bit_length() - 1
+        step = depth - 1 - high
+        gather_terms(p, k, step, None)
+        copy = pltpu.make_async_remote_copy(
+            src_ref=own.at[plan.canon(order, k), pl.ds(lo, count)],
+            dst_ref=rv[p][step].at[k - 2**high],
+            send_sem=rs_send.at[p, k],
+            recv_sem=rs_recv.at[p, k],
+            device_id=others[order[step]],
+            device_id_type=MESH,
+        )
+        copy.start()
+        sums[(p, k)] = copy
+
+    pl.semaphore_wait(barrier, 1 + depth)
+    lag = 2
+    for n in range(blocks + lag):
+        if n < blocks:
+            c = sequence[n]
+            send_term(c)
+            own[c] = term(0, c)
+        if n >= lag:
+            for p, (order, _, _) in enumerate(sum_parts):
+                for k in range(blocks - 1, blocks // 2 - 1, -1):
+                    if plan.canon(order, k) == sequence[n - lag]:
+                        send_sum(p, k)
+    for k in range(blocks // 2 - 1, 0, -1):
+        for p in range(len(sum_parts)):
+            send_sum(p, k)
+    for p in range(len(sum_parts)):
+        gather_terms(p, 0, depth, total)
+
+    def update(lo, count):
+        gradient = total[:, lo : lo + count].T
+        span = pl.ds(lo, count)
         master, first, second = adamw_update(gradient, mw[span, :], m1[span, :], m2[span, :])
         nm[span, :] = master
         n1[span, :] = first
         n2[span, :] = second
         weights[0, 0, span, :] = master.astype(BF16)
 
-    stores = [
-        pltpu.make_async_copy(s, d, local.at[6 + i])
-        for i, (s, d) in enumerate([(nm, nm_o), (n1, n1_o), (n2, n2_o)])
-    ]
-    for store in stores:
-        store.start()
-
-    acc[...] = jnp.zeros_like(acc)
-    loads[5].wait()
+    for load in loads[:3]:
+        load.wait()
 
     def project(side, c):
         acc[...] += jnp.dot(
@@ -256,15 +281,16 @@
     pending = []
 
     def finish_sibling(c):
-        for p in range(n_parts):
+        for p in range(len(keep_parts)):
             crossed[(p, c)].wait_recv()
         project(1, c)
 
     for q in range(blocks):
         ready = []
-        for p in range(n_parts):
-            order, _, (lo, count) = plan.parts[p]
-            c = plan.canon(p, q)
+        for p, (order, lo, count) in enumerate(keep_parts):
+            c = plan.canon(order, q)
+            if q == 0:
+                update(lo, count)
             high = q.bit_length() - 1
             if q > 0:
                 passed[(p, q - 2**high, high)].wait_recv()
@@ -292,15 +318,24 @@
             copy.start()
             crossed[(p, c)] = copy
             have[c] += 1
-            if have[c] == n_parts:
+            if have[c] == len(keep_parts):
                 ready.append(c)
+        if q == 0:
+            stores = [
+                pltpu.make_async_copy(s, d, local.at[5 + i])
+                for i, (s, d) in enumerate([(nm, nm_o), (n1, n1_o), (n2, n2_o)])
+            ]
+            for store in stores:
+                store.start()
+            acc[...] = jnp.zeros_like(acc)
+            loads[3].wait()
         for c in ready:
             if c & inner_mask == 0:
                 o, _ = block_at(False, c)
                 keep = pltpu.make_async_copy(
                     weights.at[0, c],
                     kept_o.at[pl.ds(pl.multiple_of(o * R, R), R)],
-                    local.at[9 + len(keeps)],
+                    local.at[8 + len(keeps)],
                 )
                 keep.start()
                 keeps.append(keep)
@@ -312,9 +347,7 @@
         finish_sibling(c)
     proj_o[...] = acc[...].astype(BF16)
 
-    for c in range(blocks):
-        core_copy(c).wait_send()
-    for copy in list(sums.values()) + list(passed.values()) + list(crossed.values()):
+    for copy in list(cores.values()) + list(sums.values()) + list(passed.values()) + list(crossed.values()):
         copy.wait_send()
     for copy in stores + keeps:
         copy.wait()
@@ -326,15 +359,16 @@
     next_rows = next_tokens.shape[0]
     R, C = master_weights.shape
     plan = Plan(n_out, n_in, R, C)
-    B, L, n_parts = plan.blocks, plan.depth, len(plan.parts)
+    B, L = plan.blocks, plan.depth
+    n_sum, n_keep = len(plan.sum_parts), len(plan.keep_parts)
     dma = pltpu.SemaphoreType.DMA
     any_spec = pl.BlockSpec(memory_space=pl.ANY)
     arrived = [
         pltpu.VMEM((2 ** (L - 1 - s), count, R), BF16)
-        for _, (_, count), _ in plan.parts
+        for _, _, count in plan.sum_parts
         for s in range(L)
     ]
-    return pl.pallas_call(
+    results = pl.pallas_call(
         functools.partial(kernel, plan),
         out_shape=(
             jax.ShapeDtypeStruct((R, C), F32),
@@ -346,7 +380,7 @@
         in_specs=[any_spec] * 6,
         out_specs=(any_spec,) * 4 + (pl.BlockSpec(memory_space=pltpu.VMEM),),
         scratch_shapes=[
-            pltpu.VMEM((tokens, width), BF16),
+            pltpu.VMEM((2, B, tokens, R), BF16),
             pltpu.VMEM((tokens, C), BF16),
             pltpu.VMEM((next_rows, width), BF16),
         ]
@@ -362,15 +396,16 @@
         ]
         + arrived
         + [
+            dma((2, B)),
             dma((B,)),
             dma((B,)),
-            dma((n_parts, B)),
-            dma((n_parts, B)),
-            dma((n_parts, B)),
-            dma((n_parts, B)),
-            dma((n_parts, B)),
-            dma((n_parts, B)),
-            dma((9 + n_out,)),
+            dma((n_sum, B)),
+            dma((n_sum, B)),
+            dma((n_keep, B)),
+            dma((n_keep, B)),
+            dma((n_keep, B)),
+            dma((n_keep, B)),
+            dma((8 + n_out,)),
         ],
         compiler_params=pltpu.CompilerParams(
             collective_id=0, has_side_effects=True, vmem_limit_bytes=58 * 2**20
@@ -381,6 +416,29 @@
             transcendentals=R * C,
         ),
     )(activations, output_grads, master_weights, first_moment, second_moment, next_tokens)
+    return hand_on(results)
+
+
+def copy_kernel(*refs):
+    count = len(refs) // 2
+    copies = [
+        pltpu.make_async_copy(refs[i], refs[count + i], refs[-1].at[i]) for i in range(count)
+    ]
+    for copy in copies:
+        copy.start()
+    for copy in copies:
+        copy.wait()
+
+
+def hand_on(arrays):
+    any_spec = pl.BlockSpec(memory_space=pl.ANY)
+    return pl.pallas_call(
+        copy_kernel,
+        out_shape=tuple(jax.ShapeDtypeStruct(a.shape, a.dtype) for a in arrays),
+        in_specs=[any_spec] * len(arrays),
+        out_specs=(any_spec,) * len(arrays),
+        scratch_shapes=[pltpu.SemaphoreType.DMA((len(arrays),))],
+    )(*arrays)
 
 
 def fits_kernel(mesh):

time: 111 us -> 206 us (1.86)
  Pallas kernels: 102 us -> 205 us
  local copies, waits for them, and re-layouts: 7.78 us -> 0 us
    pallas_call x0 -> x1, Pallas kernels: none -> 120 us  [hand_on(): pl.pallas_call(copy_kernel, out_shape=tuple((jax.ShapeDtypeStruct(a.shape...]
    pallas_call x1, Pallas kernels: 102 us -> 85.1 us  [local_kernel(): pl.pallas_call(functools.partial(kernel, plan), out_shape=(jax.ShapeDtype...]
    unnamed x9 -> x0, local copies, waits for them, and re-layouts: 7.78 us -> none
where the time goes in v2:
time: 206 us
  Pallas kernels  205 us (100%)
    pallas_call x1, Pallas kernels, hand_on(): pl.pallas_call(copy_kernel, out_shape=tuple((jax.ShapeDtypeStruct(a.shape...  120 us
    pallas_call x1, Pallas kernels, local_kernel(): pl.pallas_call(functools.partial(kernel, plan), out_shape=(jax.ShapeDtype...  85.1 us

profile of v2, /device:TPU:1, one launch (start us, length us, event | category | flops | bytes accessed | tf_op | source)
XLA Modules:
  0.0 206.0 jit_solution(9988683226317811327)
XLA Ops:
  0.6 85.1 %shard_map.101 = (f32[256,512]{1,0:T(8,128)}, f32[256,512]{1,0:T(8,128)}, f32[256,512]{1,0:T(8,128)}, bf16[2048,512]{1,0:T(8,128)(2,1)}, bf16[256,512]{1,0:T(8,128)(2,1)}) custom-call(bf16[256,8192]{1,0:T(8,128)(2,1)} %refs_0_.1, bf16[256,512]{1,0:T(8,128)(2,1)} %refs_1_.1, f32[256,512]{1,0:T(8,128)} %refs_2_.1, f32[256,512]{1,0:T(8,128)} %refs_3_.1, ...), custom_call_target="tpu_custom_call" | custom-call | flops 4294967296 | bytes 11534336 | tf_op jit(solution)/shard_map/pallas_call | solution.py:371
  85.8 120.3 %shard_map.102 = (f32[256,512]{1,0:T(8,128)}, f32[256,512]{1,0:T(8,128)}, f32[256,512]{1,0:T(8,128)}, bf16[2048,512]{1,0:T(8,128)(2,1)}, bf16[256,512]{1,0:T(8,128)(2,1)}) custom-call(f32[256,512]{1,0:T(8,128)} %get-tuple-element.10.refs_0_, f32[256,512]{1,0:T(8,128)} %get-tuple-element.11.refs_1_, f32[256,512]{1,0:T(8,128)} %get-tuple-element.12.refs_2_, ...), custom_call_target="tpu_custom_call" | custom-call | tf_op jit(solution)/shard_map/pallas_call | solution.py:435

commit v3 on v2

--- a/solution.py
+++ b/solution.py
@@ -419,25 +419,41 @@
     return hand_on(results)
 
 
-def copy_kernel(*refs):
-    count = len(refs) // 2
-    copies = [
-        pltpu.make_async_copy(refs[i], refs[count + i], refs[-1].at[i]) for i in range(count)
+def copy_kernel(pieces, *refs):
+    count = len(refs) // 3
+    sources, targets, held, sems = refs[:count], refs[count : 2 * count], refs[2 * count : -1], refs[-1]
+    spans = [
+        (i, pl.ds(n * (ref.shape[0] // pieces), ref.shape[0] // pieces))
+        for i, ref in enumerate(sources)
+        for n in range(pieces)
     ]
-    for copy in copies:
+    ins = [
+        pltpu.make_async_copy(sources[i].at[at], held[i].at[at], sems.at[0, n])
+        for n, (i, at) in enumerate(spans)
+    ]
+    outs = [
+        pltpu.make_async_copy(held[i].at[at], targets[i].at[at], sems.at[1, n])
+        for n, (i, at) in enumerate(spans)
+    ]
+    for copy in ins:
         copy.start()
-    for copy in copies:
+    for copy, onward in zip(ins, outs):
         copy.wait()
-
-
-def hand_on(arrays):
+        onward.start()
+    for copy in outs:
+        copy.wait()
+
+
+def hand_on(arrays, pieces=2):
     any_spec = pl.BlockSpec(memory_space=pl.ANY)
     return pl.pallas_call(
-        copy_kernel,
+        functools.partial(copy_kernel, pieces),
         out_shape=tuple(jax.ShapeDtypeStruct(a.shape, a.dtype) for a in arrays),
         in_specs=[any_spec] * len(arrays),
         out_specs=(any_spec,) * len(arrays),
-        scratch_shapes=[pltpu.SemaphoreType.DMA((len(arrays),))],
+        scratch_shapes=[pltpu.VMEM(a.shape, a.dtype) for a in arrays]
+        + [pltpu.SemaphoreType.DMA((2, pieces * len(arrays)))],
+        compiler_params=pltpu.CompilerParams(vmem_limit_bytes=48 * 2**20),
     )(*arrays)
 
 

time: 206 us -> 94.4 us (0.46)
  Pallas kernels: 205 us -> 87.8 us
  local copies, waits for them, and re-layouts: 0 us -> 5.66 us
    pallas_call x1, Pallas kernels: 120 us -> 2.66 us  [hand_on(): pl.pallas_call(functools.partial(copy_kernel, pieces), out_shape=tuple((j...]
    unnamed x0 -> x10, local copies, waits for them, and re-layouts: none -> 5.66 us
where the time goes in v3:
time: 94.4 us; the launch traced here: 94.1 us
  Pallas kernels  87.8 us (93%)
  local copies, waits for them, and re-layouts  5.66 us (6%)
    pallas_call x1, Pallas kernels, local_kernel(): pl.pallas_call(functools.partial(kernel, plan), out_shape=(jax.ShapeDtype...  85.1 us
    unnamed x10, local copies, waits for them, and re-layouts  5.66 us
    pallas_call x1, Pallas kernels, hand_on(): pl.pallas_call(functools.partial(copy_kernel, pieces), out_shape=tuple((j...  2.66 us

profile of v3, /device:TPU:1, one launch (start us, length us, event | category | flops | bytes accessed | tf_op | source)
XLA Modules:
  0.0 94.1 jit_solution(17833822549464568905)
XLA Ops:
  0.6 85.1 %shard_map.101 = (f32[256,512]{1,0:T(8,128)}, f32[256,512]{1,0:T(8,128)}, f32[256,512]{1,0:T(8,128)}, bf16[2048,512]{1,0:T(8,128)(2,1)}, bf16[256,512]{1,0:T(8,128)(2,1)}) custom-call(bf16[256,8192]{1,0:T(8,128)(2,1)} %refs_0_.1, bf16[256,512]{1,0:T(8,128)(2,1)} %refs_1_.1, f32[256,512]{1,0:T(8,128)} %refs_2_.1, f32[256,512]{1,0:T(8,128)} %refs_3_.1, ...), custom_call_target="tpu_custom_call" | custom-call | flops 4294967296 | bytes 11534336 | tf_op jit(solution)/shard_map/pallas_call | solution.py:371
  85.8 0.0 copy-start
  85.8 1.6 %copy-done = bf16[2048,512]{1,0:T(8,128)(2,1)S(1)} copy-done((bf16[2048,512]{1,0:T(8,128)(2,1)S(1)}, bf16[2048,512]{1,0:T(8,128)(2,1)}, u32[]{:S(2)}) %copy-start) | copy-done | bytes 2097176
  87.3 0.0 copy-start.1
  87.3 1.0 %copy-done.1 = f32[256,512]{1,0:T(8,128)S(1)} copy-done((f32[256,512]{1,0:T(8,128)S(1)}, f32[256,512]{1,0:T(8,128)}, u32[]{:S(2)}) %copy-start.1) | copy-done | bytes 524312
  88.4 0.0 copy-start.2
  88.4 1.0 %copy-done.2 = f32[256,512]{1,0:T(8,128)S(1)} copy-done((f32[256,512]{1,0:T(8,128)S(1)}, f32[256,512]{1,0:T(8,128)}, u32[]{:S(2)}) %copy-start.2) | copy-done | bytes 524312
  89.4 0.0 copy-start.3
  89.4 1.0 %copy-done.3 = f32[256,512]{1,0:T(8,128)S(1)} copy-done((f32[256,512]{1,0:T(8,128)S(1)}, f32[256,512]{1,0:T(8,128)}, u32[]{:S(2)}) %copy-start.3) | copy-done | bytes 524312
  90.5 0.0 copy-start.4
  90.5 0.9 %copy-done.4 = bf16[256,512]{1,0:T(8,128)(2,1)S(1)} copy-done((bf16[256,512]{1,0:T(8,128)(2,1)S(1)}, bf16[256,512]{1,0:T(8,128)(2,1)}, u32[]{:S(2)}) %copy-start.4) | copy-done | bytes 262168
  91.4 2.7 %shard_map.102 = (f32[256,512]{1,0:T(8,128)}, f32[256,512]{1,0:T(8,128)}, f32[256,512]{1,0:T(8,128)}, bf16[2048,512]{1,0:T(8,128)(2,1)}, bf16[256,512]{1,0:T(8,128)(2,1)}) custom-call(f32[256,512]{1,0:T(8,128)S(1)} %copy-done.1, f32[256,512]{1,0:T(8,128)S(1)} %copy-done.2, f32[256,512]{1,0:T(8,128)S(1)} %copy-done.3, bf16[2048,512]{1,0:T(8,128)(2,1)S(1)} %copy-done, ...), custom_call_target="tpu_custom_call" | custom-call | tf_op jit(solution)/shard_map/pallas_call | solution.py:449
Async XLA Ops:
  85.8 1.6 %copy-start = (bf16[2048,512]{1,0:T(8,128)(2,1)S(1)}, bf16[2048,512]{1,0:T(8,128)(2,1)}, u32[]{:S(2)}) copy-start(bf16[2048,512]{1,0:T(8,128)(2,1)} %get-tuple-element.13.refs_3_) | copy-start | bytes 6291460
  87.3 1.0 %copy-start.1 = (f32[256,512]{1,0:T(8,128)S(1)}, f32[256,512]{1,0:T(8,128)}, u32[]{:S(2)}) copy-start(f32[256,512]{1,0:T(8,128)} %get-tuple-element.10.refs_0_) | copy-start | bytes 1572868
  88.4 1.0 %copy-start.2 = (f32[256,512]{1,0:T(8,128)S(1)}, f32[256,512]{1,0:T(8,128)}, u32[]{:S(2)}) copy-start(f32[256,512]{1,0:T(8,128)} %get-tuple-element.11.refs_1_) | copy-start | bytes 1572868
  89.4 1.0 %copy-start.3 = (f32[256,512]{1,0:T(8,128)S(1)}, f32[256,512]{1,0:T(8,128)}, u32[]{:S(2)}) copy-start(f32[256,512]{1,0:T(8,128)} %get-tuple-element.12.refs_2_) | copy-start | bytes 1572868
  90.5 0.9 %copy-start.4 = (bf16[256,512]{1,0:T(8,128)(2,1)S(1)}, bf16[256,512]{1,0:T(8,128)(2,1)}, u32[]{:S(2)}) copy-start(bf16[256,512]{1,0:T(8,128)(2,1)} %get-tuple-element.14.refs_4_) | copy-start | bytes 786436

commit v4 on v3

v4 whole, which is shorter than its diff:
```python
import functools

import jax
import jax.numpy as jnp
from jax import lax
from jax.experimental import pallas as pl
from jax.experimental.pallas import tpu as pltpu
from jax.sharding import PartitionSpec as P

ADAM_STEP = 10
MESH = pl.DeviceIdType.MESH
BF16 = jnp.bfloat16
F32 = jnp.float32


beta_first = 0.9
beta_second = 0.95
learn_rate = 0.002
decay_rate = 0.1
adam_eps = 1e-08


def adamw_update(gradient, master_weights, first_moment, second_moment):
    new_first = beta_first * first_moment + (1.0 - beta_first) * gradient
    new_second = beta_second * second_moment + (1.0 - beta_second) * gradient * gradient
    first_hat = new_first / (1.0 - beta_first**ADAM_STEP)
    second_hat = new_second / (1.0 - beta_second**ADAM_STEP)
    new_master = master_weights - learn_rate * (
        first_hat / (jnp.sqrt(second_hat) + adam_eps) + decay_rate * master_weights
    )
    return (new_master, new_first, new_second)


def rounded_term(columns, output_grads):
    contrib = jnp.einsum(
        "tr,tc->rc", columns, output_grads, preferred_element_type=jnp.float32
    ).astype(jnp.bfloat16)
    contrib = lax.optimization_barrier(contrib)
    return contrib.astype(jnp.float32)


def regroup_features(activations, outer_count, inner_count):
    tok_rows, width = activations.shape
    shard_rows = width // (outer_count * inner_count)
    split_view = activations.reshape(tok_rows, inner_count, outer_count, shard_rows)
    return split_view.transpose(0, 2, 1, 3).reshape(tok_rows, width)


def local_plain(activations, output_grads, master_weights, first_moment, second_moment, next_tokens):
    outer_count = lax.axis_size("outer")
    inner_count = lax.axis_size("inner")
    regrouped = regroup_features(activations, outer_count, inner_count)
    gradient = lax.psum_scatter(
        rounded_term(regrouped, output_grads), ("outer", "inner"), scatter_dimension=0, tiled=True
    )
    new_master, new_first, new_second = adamw_update(
        gradient, master_weights, first_moment, second_moment
    )
    kept_shard = new_master.astype(jnp.bfloat16)
    kept_weights = lax.all_gather(kept_shard, "outer", axis=0, tiled=True)
    projected = jnp.dot(
        next_tokens,
        lax.all_gather(kept_weights, "inner", axis=0, tiled=True),
        preferred_element_type=jnp.float32,
    )
    return (new_master, new_first, new_second, kept_weights, projected.astype(jnp.bfloat16))


SUM_ORDERS = [
    [(3, 2, 1, 0), (2, 3, 1, 0)],
    [(3, 2, 1, 0), (2, 3, 1, 0)],
]
GATHER_ORDERS = [
    [(3, 2, 1, 0), (2, 3, 1, 0)],
    [(3, 2, 1, 0), (2, 3, 1, 0)],
]
STEPS = [
    ("T", 0, 15), ("T", 0, 14), ("T", 0, 13), ("T", 0, 12), ("T", 0, 11), ("S", 0, 0, 15),
    ("S", 0, 1, 15), ("S", 0, 0, 14), ("S", 0, 1, 14), ("S", 0, 0, 13), ("S", 0, 1, 13),
    ("S", 0, 0, 12), ("S", 0, 1, 12), ("T", 0, 7), ("S", 0, 0, 11), ("T", 0, 10), ("T", 0, 6),
    ("T", 0, 9), ("S", 0, 1, 11), ("S", 0, 0, 7), ("S", 0, 1, 7), ("T", 0, 5), ("S", 0, 0, 10),
    ("S", 0, 1, 10), ("S", 0, 0, 6), ("S", 0, 0, 9), ("S", 0, 1, 6), ("T", 0, 8), ("T", 0, 4),
    ("S", 0, 1, 9), ("S", 0, 0, 5), ("S", 0, 1, 5), ("T", 0, 3), ("T", 0, 2), ("S", 0, 0, 8),
    ("S", 0, 1, 8), ("S", 0, 0, 4), ("S", 0, 1, 4), ("T", 0, 1), ("T", 0, 0), ("T", 1, 15),
    ("T", 1, 14), ("T", 1, 13), ("S", 0, 0, 3), ("S", 0, 1, 3), ("T", 1, 12), ("S", 1, 0, 15),
    ("S", 1, 1, 15), ("S", 1, 0, 14), ("S", 1, 1, 14), ("S", 1, 0, 13), ("S", 1, 1, 13),
    ("T", 1, 11), ("S", 1, 0, 12), ("S", 1, 1, 12), ("T", 1, 7), ("S", 0, 0, 2), ("T", 1, 10),
    ("T", 1, 6), ("S", 1, 0, 11), ("S", 0, 1, 2), ("T", 1, 9), ("S", 1, 1, 11), ("T", 1, 5),
    ("S", 1, 0, 10), ("S", 1, 1, 10), ("S", 0, 1, 1), ("S", 0, 0, 1), ("T", 1, 8), ("S", 1, 0, 9),
    ("T", 1, 4), ("S", 1, 1, 9), ("T", 1, 3), ("T", 1, 2), ("S", 1, 0, 8), ("T", 1, 1),
    ("S", 1, 1, 8), ("T", 1, 0), ("S", 1, 0, 7), ("S", 1, 1, 7), ("S", 1, 0, 6), ("S", 1, 1, 6),
    ("F", 0), ("A", 0, 0, 0), ("A", 0, 1, 0), ("S", 1, 0, 5), ("S", 1, 1, 5), ("S", 1, 0, 4),
    ("S", 1, 1, 4), ("D", 0, 0, 0), ("A", 0, 0, 1), ("D", 1, 0, 0), ("A", 0, 0, 2),
    ("A", 0, 1, 2), ("D", 0, 0, 2), ("A", 0, 1, 1), ("D", 0, 0, 1), ("D", 1, 0, 2),
    ("S", 1, 1, 3), ("S", 1, 0, 3), ("D", 1, 0, 1), ("S", 1, 1, 2), ("S", 1, 0, 2),
    ("A", 0, 0, 3), ("A", 0, 0, 8), ("A", 0, 0, 4), ("A", 0, 1, 4), ("A", 0, 1, 8),
    ("D", 0, 0, 4), ("D", 0, 0, 8), ("D", 1, 0, 8), ("S", 1, 1, 1), ("A", 0, 1, 3),
    ("S", 1, 0, 1), ("D", 0, 0, 3), ("D", 1, 0, 4), ("D", 1, 0, 3), ("A", 0, 0, 9),
    ("A", 0, 0, 5), ("A", 0, 0, 10), ("A", 0, 0, 6), ("A", 0, 1, 6), ("A", 0, 1, 10),
    ("D", 0, 0, 6), ("D", 0, 0, 10), ("F", 1), ("A", 0, 1, 5), ("A", 0, 0, 7), ("A", 0, 1, 9),
    ("A", 0, 0, 11), ("A", 1, 0, 0), ("A", 1, 1, 0), ("A", 0, 0, 12), ("A", 0, 1, 12),
    ("D", 0, 0, 5), ("D", 1, 0, 5), ("D", 1, 0, 6), ("D", 0, 0, 9), ("D", 1, 0, 9),
    ("D", 1, 0, 10), ("D", 0, 0, 12), ("A", 0, 1, 7), ("A", 0, 1, 11), ("D", 0, 0, 7),
    ("D", 0, 0, 11), ("D", 1, 0, 12), ("D", 0, 1, 0), ("D", 1, 1, 0), ("A", 1, 0, 2),
    ("A", 0, 0, 13), ("D", 1, 0, 11), ("A", 0, 1, 14), ("A", 1, 0, 1), ("D", 1, 0, 7),
    ("A", 0, 0, 14), ("D", 0, 0, 14), ("A", 0, 1, 13), ("D", 0, 0, 13), ("A", 1, 1, 2),
    ("D", 0, 1, 2), ("D", 1, 0, 14), ("A", 0, 0, 15), ("A", 1, 0, 4), ("A", 1, 1, 1),
    ("D", 1, 0, 13), ("D", 0, 1, 1), ("D", 1, 1, 2), ("A", 1, 0, 8), ("A", 1, 1, 8),
    ("D", 0, 1, 4), ("D", 1, 1, 1), ("A", 1, 0, 3), ("A", 1, 1, 4), ("A", 0, 1, 15),
    ("D", 0, 0, 15), ("D", 1, 1, 4), ("D", 0, 1, 8), ("A", 1, 1, 3), ("D", 0, 1, 3),
    ("D", 1, 1, 8), ("A", 1, 0, 10), ("A", 1, 0, 6), ("D", 1, 0, 15), ("D", 1, 1, 3),
    ("A", 1, 0, 9), ("A", 1, 0, 5), ("A", 1, 1, 6), ("A", 1, 1, 10), ("D", 0, 1, 6),
    ("D", 0, 1, 10), ("D", 1, 1, 10), ("A", 1, 0, 12), ("A", 1, 1, 9), ("D", 0, 1, 5),
    ("D", 1, 1, 6), ("A", 1, 1, 5), ("A", 1, 0, 7), ("D", 1, 1, 5), ("D", 0, 1, 9),
    ("D", 1, 1, 9), ("A", 1, 0, 11), ("A", 1, 1, 12), ("D", 0, 1, 12), ("A", 1, 1, 7),
    ("A", 1, 1, 11), ("D", 0, 1, 7), ("D", 0, 1, 11), ("D", 1, 1, 12), ("D", 1, 1, 11),
    ("A", 1, 0, 14), ("A", 1, 1, 14), ("D", 1, 1, 7), ("D", 0, 1, 14), ("A", 1, 0, 13),
    ("A", 1, 1, 13), ("D", 0, 1, 13), ("D", 1, 1, 14), ("A", 1, 0, 15), ("D", 1, 1, 13),
    ("A", 1, 1, 15), ("D", 0, 1, 15), ("D", 1, 1, 15),
]


class Plan:
    def __init__(self, n_out, n_in, rows, cols):
        self.n_out, self.n_in, self.rows, self.cols = n_out, n_in, rows, cols
        out_bits = [("outer", k) for k in range(n_out.bit_length() - 1)]
        in_bits = [("inner", k) for k in range(1, n_in.bit_length() - 1)]
        ranked = []
        for k in range(max(len(out_bits), len(in_bits))):
            ranked += out_bits[k : k + 1] + in_bits[k : k + 1]
        self.dims = ranked[::-1]
        self.depth = len(ranked)
        self.blocks = 2**self.depth
        self.groups = len(SUM_ORDERS)
        self.parts = len(SUM_ORDERS[0])
        self.group_cols = cols // self.groups

    def canon(self, order, k):
        return sum(((k >> t) & 1) << order[self.depth - 1 - t] for t in range(self.depth))


def kernel(plan, *refs):
    (act_h, grad_h, mw_h, m1_h, m2_h, nt_h, nm_o, n1_o, n2_o, kept_o, proj_o) = refs[:11]
    (act, grad, nt, mw, m1, m2, nm, n1, n2, grad_t, own, snd0, rcv0, total, weights, acc) = refs[11:27]
    depth, blocks, groups, parts = plan.depth, plan.blocks, plan.groups, plan.parts
    rv_flat = refs[27 : 27 + groups * parts * depth]
    (
        load_sem,
        core_send,
        core_recv,
        rs_send,
        rs_recv,
        ag_send,
        ag_recv,
        cg_send,
        cg_recv,
        local,
        group_local,
    ) = refs[27 + groups * parts * depth :]
    rv = {
        (g, p): rv_flat[(g * parts + p) * depth : (g * parts + p + 1) * depth]
        for g in range(groups)
        for p in range(parts)
    }
    wide = plan.group_cols
    R, C = plan.rows, plan.cols

    outer, inner = lax.axis_index("outer"), lax.axis_index("inner")
    place = {"outer": outer, "inner": inner}

    def bit(axis, k):
        return (place[axis] // 2**k) % 2

    def partner(axis, k):
        other = place[axis] + (1 - 2 * bit(axis, k)) * 2**k
        return (other, inner) if axis == "outer" else (outer, other)

    sibling = partner("inner", 0)
    others = [partner(axis, k) for axis, k in plan.dims]

    barrier = pltpu.get_barrier_semaphore()
    for device in [sibling] + others:
        pl.semaphore_signal(barrier, inc=1, device_id=device, device_id_type=MESH)

    def block_at(flip_core, c):
        o, n = outer, inner
        if flip_core:
            n = n + 1 - 2 * bit("inner", 0)
        for j, (axis, k) in enumerate(plan.dims):
            step = ((c // 2**j) % 2) * (1 - 2 * bit(axis, k)) * 2**k
            if axis == "outer":
                o = o + step
            else:
                n = n + step
        return o, n

    def columns(flip_core, c):
        o, n = block_at(flip_core, c)
        return pl.ds(pl.multiple_of((n * plan.n_out + o) * R, R), R)

    sequence = [step[2] for step in STEPS if step[0] == "T" and step[1] == 0]

    first_load = pltpu.make_async_copy(grad_h, grad, local.at[0])
    first_load.start()
    act_loads = {}
    for c in sequence:
        for side in (1, 0):
            load = pltpu.make_async_copy(
                act_h.at[:, columns(side == 1, c)], act.at[side, c], load_sem.at[side, c]
            )
            load.start()
            act_loads[(side, c)] = load
    loads = [
        pltpu.make_async_copy(s, d, local.at[1 + i])
        for i, (s, d) in enumerate([(mw_h, mw), (m1_h, m1), (m2_h, m2), (nt_h, nt)])
    ]
    for load in loads:
        load.start()

    first_load.wait()
    grad_t[...] = grad[...].astype(F32).T.astype(BF16)
    pl.semaphore_wait(barrier, 1 + depth)

    cores, sums, passed, crossed, stores = {}, {}, {}, {}, []
    done = set()

    def once(key, wait):
        if key not in done:
            done.add(key)
            wait()

    def group_span(g):
        return pl.ds(g * wide, wide)

    def term(side, g, c):
        once(("act", side, c), act_loads[(side, c)].wait)
        return jnp.dot(
            grad_t[group_span(g), :], act[side, c], preferred_element_type=F32
        ).astype(BF16)

    def send_term(g, c):
        at = (c, group_span(g))
        snd0[c, group_span(g), :] = term(1, g, c)
        copy = pltpu.make_async_remote_copy(
            src_ref=snd0.at[at],
            dst_ref=rcv0.at[at],
            send_sem=core_send.at[g, c],
            recv_sem=core_recv.at[g, c],
            device_id=sibling,
            device_id_type=MESH,
        )
        copy.start()
        cores[(g, c)] = copy
        own[c, group_span(g), :] = term(0, g, c)

    count = wide // parts
    tile = min(count, 64)

    def gather_terms(g, p, k, steps, last):
        c = plan.canon(SUM_ORDERS[g][p], k)
        once(("core", g, c), cores[(g, c)].wait_recv)
        for t in range(steps):
            sums[(g, p, k + 2 ** (depth - 1 - t))].wait_recv()
        for at in range(0, count, tile):
            span = pl.ds(g * wide + p * count + at, tile)
            value = own[c, span, :].astype(F32) + rcv0[c, span, :].astype(F32)
            for t in range(steps):
                value += rv[(g, p)][t][k, pl.ds(at, tile), :].astype(F32)
            if last:
                total[span, :] = value
            else:
                own[c, span, :] = value.astype(BF16)

    def send_sum(g, p, k):
        order = SUM_ORDERS[g][p]
        high = k.bit_length() - 1
        step = depth - 1 - high
        gather_terms(g, p, k, step, False)
        copy = pltpu.make_async_remote_copy(
            src_ref=own.at[plan.canon(order, k), pl.ds(g * wide + p * count, count)],
            dst_ref=rv[(g, p)][step].at[k - 2**high],
            send_sem=rs_send.at[g * parts + p, k],
            recv_sem=rs_recv.at[g * parts + p, k],
            device_id=others[order[step]],
            device_id_type=MESH,
        )
        copy.start()
        sums[(g, p, k)] = copy

    def update(g):
        for p in range(parts):
            gather_terms(g, p, 0, depth, True)
        once("state", lambda: [load.wait() for load in loads[:3]])
        span = group_span(g)
        gradient = total[span, :].T
        master, first, second = adamw_update(gradient, mw[:, span], m1[:, span], m2[:, span])
        weights[0, g, 0] = master.astype(BF16)
        nm[:, span] = master
        n1[:, span] = first
        n2[:, span] = second
        for i, (s, d) in enumerate([(nm, nm_o), (n1, n1_o), (n2, n2_o)]):
            store = pltpu.make_async_copy(s.at[:, span], d.at[:, span], group_local.at[g, i])
            store.start()
            stores.append(store)

    def pass_on(g, p, q):
        order = GATHER_ORDERS[g][p]
        c = plan.canon(order, q)
        high = q.bit_length() - 1
        if q > 0:
            passed[(g, p, q)].wait_recv()
        rows = pl.ds(p * (R // parts), R // parts)
        for t in range(high + 1, depth):
            e = order[depth - 1 - t]
            copy = pltpu.make_async_remote_copy(
                src_ref=weights.at[0, g, c, rows],
                dst_ref=weights.at[0, g, c + 2**e, rows],
                send_sem=ag_send.at[g * parts + p, q + 2**t],
                recv_sem=ag_recv.at[g * parts + p, q + 2**t],
                device_id=others[e],
                device_id_type=MESH,
            )
            copy.start()
            passed[(g, p, q + 2**t)] = copy
        copy = pltpu.make_async_remote_copy(
            src_ref=weights.at[0, g, c, rows],
            dst_ref=weights.at[1, g, c, rows],
            send_sem=cg_send.at[g * parts + p, c],
            recv_sem=cg_recv.at[g * parts + p, c],
            device_id=sibling,
            device_id_type=MESH,
        )
        copy.start()
        crossed[(g, p, c)] = copy

    inner_mask = sum(2**j for j, (axis, _) in enumerate(plan.dims) if axis == "inner")

    def project(side, g, c):
        span = group_span(g)
        if side == 1:
            for p in range(parts):
                crossed[(g, p, c)].wait_recv()
        elif c & inner_mask == 0:
            o, _ = block_at(False, c)
            keep = pltpu.make_async_copy(
                weights.at[0, g, c],
                kept_o.at[pl.ds(pl.multiple_of(o * R, R), R), span],
                group_local.at[g, 3 + c],
            )
            keep.start()
            stores.append(keep)
        once("next", loads[3].wait)
        share = jnp.dot(
            nt[:, columns(side == 1, c)], weights[side, g, c], preferred_element_type=F32
        )
        if ("acc", g) in done:
            acc[:, span] += share
        else:
            done.add(("acc", g))
            acc[:, span] = share

    run = {"T": send_term, "S": send_sum, "F": update, "A": pass_on, "D": project}
    for step in STEPS:
        run[step[0]](*step[1:])
    proj_o[...] = acc[...].astype(BF16)

    for group in (cores, sums, passed, crossed):
        for copy in group.values():
            copy.wait_send()
    for copy in stores:
        copy.wait()


def local_kernel(activations, output_grads, master_weights, first_moment, second_moment, next_tokens):
    n_out, n_in = lax.axis_size("outer"), lax.axis_size("inner")
    tokens, width = activations.shape
    next_rows = next_tokens.shape[0]
    R, C = master_weights.shape
    plan = Plan(n_out, n_in, R, C)
    B, L, G, n_parts = plan.blocks, plan.depth, plan.groups, plan.groups * plan.parts
    dma = pltpu.SemaphoreType.DMA
    any_spec = pl.BlockSpec(memory_space=pl.ANY)
    arrived = [
        pltpu.VMEM((2 ** (L - 1 - s), plan.group_cols // plan.parts, R), BF16)
        for _ in range(n_parts)
        for s in range(L)
    ]
    results = pl.pallas_call(
        functools.partial(kernel, plan),
        out_shape=(
            jax.ShapeDtypeStruct((R, C), F32),
            jax.ShapeDtypeStruct((R, C), F32),
            jax.ShapeDtypeStruct((R, C), F32),
            jax.ShapeDtypeStruct((n_out * R, C), BF16),
            jax.ShapeDtypeStruct((next_rows, C), BF16),
        ),
        in_specs=[any_spec] * 6,
        out_specs=(any_spec,) * 4 + (pl.BlockSpec(memory_space=pltpu.VMEM),),
        scratch_shapes=[
            pltpu.VMEM((2, B, tokens, R), BF16),
            pltpu.VMEM((tokens, C), BF16),
            pltpu.VMEM((next_rows, width), BF16),
        ]
        + [pltpu.VMEM((R, C), F32)] * 6
        + [
            pltpu.VMEM((C, tokens), BF16),
            pltpu.VMEM((B, C, R), BF16),
            pltpu.VMEM((B, C, R), BF16),
            pltpu.VMEM((B, C, R), BF16),
            pltpu.VMEM((C, R), F32),
            pltpu.VMEM((2, G, B, R, plan.group_cols), BF16),
            pltpu.VMEM((next_rows, C), F32),
        ]
        + arrived
        + [
            dma((2, B)),
            dma((G, B)),
            dma((G, B)),
            dma((n_parts, B)),
            dma((n_parts, B)),
            dma((n_parts, B)),
            dma((n_parts, B)),
            dma((n_parts, B)),
            dma((n_parts, B)),
            dma((5,)),
            dma((G, 3 + B)),
        ],
        compiler_params=pltpu.CompilerParams(
            collective_id=0, has_side_effects=True, vmem_limit_bytes=58 * 2**20
        ),
        cost_estimate=pl.CostEstimate(
            flops=2 * (tokens + next_rows) * width * C,
            bytes_accessed=2 * (tokens + next_rows) * width + 24 * R * C,
            transcendentals=R * C,
        ),
    )(activations, output_grads, master_weights, first_moment, second_moment, next_tokens)
    return hand_on(results)


def copy_kernel(pieces, *refs):
    count = len(refs) // 3
    sources, targets, held, sems = refs[:count], refs[count : 2 * count], refs[2 * count : -1], refs[-1]
    spans = [
        (i, pl.ds(n * (ref.shape[0] // pieces), ref.shape[0] // pieces))
        for i, ref in enumerate(sources)
        for n in range(pieces)
    ]
    ins = [
        pltpu.make_async_copy(sources[i].at[at], held[i].at[at], sems.at[0, n])
        for n, (i, at) in enumerate(spans)
    ]
    outs = [
        pltpu.make_async_copy(held[i].at[at], targets[i].at[at], sems.at[1, n])
        for n, (i, at) in enumerate(spans)
    ]
    for copy in ins:
        copy.start()
    for copy, onward in zip(ins, outs):
        copy.wait()
        onward.start()
    for copy in outs:
        copy.wait()


def hand_on(arrays, pieces=2):
    any_spec = pl.BlockSpec(memory_space=pl.ANY)
    return pl.pallas_call(
        functools.partial(copy_kernel, pieces),
        out_shape=tuple(jax.ShapeDtypeStruct(a.shape, a.dtype) for a in arrays),
        in_specs=[any_spec] * len(arrays),
        out_specs=(any_spec,) * len(arrays),
        scratch_shapes=[pltpu.VMEM(a.shape, a.dtype) for a in arrays]
        + [pltpu.SemaphoreType.DMA((2, pieces * len(arrays)))],
        compiler_params=pltpu.CompilerParams(vmem_limit_bytes=60 * 2**20),
    )(*arrays)


def fits_kernel(mesh):
    n_out, n_in = mesh.shape["outer"], mesh.shape["inner"]
    return n_out == 8 and n_in == 4


def solution(mesh):
    placed = (
        P(("outer", "inner"), None),
        P(("outer", "inner"), None),
        P(("inner", "outer"), None),
        P(("inner", "outer"), None),
        P(("inner", "outer"), None),
        P(("outer", "inner"), None),
    )
    return jax.shard_map(
        local_kernel if fits_kernel(mesh) else local_plain,
        mesh=mesh,
        in_specs=placed,
        out_specs=(
            P(("inner", "outer"), None),
            P(("inner", "outer"), None),
            P(("inner", "outer"), None),
            P("inner", None),
            P(("outer", "inner"), None),
        ),
        check_vma=False,
    )
```

time: 94.4 us -> 87.5 us (0.927)
  local copies, waits for them, and re-layouts: 5.66 us -> 0 us
  Pallas kernels: 87.8 us -> 86.6 us
    unnamed x10 -> x0, local copies, waits for them, and re-layouts: 5.66 us -> none
    pallas_call x1, Pallas kernels: 85.1 us -> 83.1 us  [local_kernel(): pl.pallas_call(functools.partial(kernel, plan), out_shape=(jax.ShapeDtype...]
where the time goes in v4:
time: 87.5 us; the launch traced here: 87.3 us
  Pallas kernels  86.6 us (99%)
    pallas_call x1, Pallas kernels, local_kernel(): pl.pallas_call(functools.partial(kernel, plan), out_shape=(jax.ShapeDtype...  83.1 us
    pallas_call x1, Pallas kernels, hand_on(): pl.pallas_call(functools.partial(copy_kernel, pieces), out_shape=tuple((j...  3.58 us

profile of v4, /device:TPU:1, one launch (start us, length us, event | category | flops | bytes accessed | tf_op | source)
XLA Modules:
  0.0 87.3 jit_solution(12129616383232103091)
XLA Ops:
  0.6 83.1 %shard_map.101 = (f32[256,512]{1,0:T(8,128)}, f32[256,512]{1,0:T(8,128)}, f32[256,512]{1,0:T(8,128)}, bf16[2048,512]{1,0:T(8,128)(2,1)}, bf16[256,512]{1,0:T(8,128)(2,1)}) custom-call(bf16[256,8192]{1,0:T(8,128)(2,1)} %refs_0_.1, bf16[256,512]{1,0:T(8,128)(2,1)} %refs_1_.1, f32[256,512]{1,0:T(8,128)} %refs_2_.1, f32[256,512]{1,0:T(8,128)} %refs_3_.1, ...), custom_call_target="tpu_custom_call" | custom-call | flops 4294967296 | bytes 11534336 | tf_op jit(solution)/shard_map/pallas_call | solution.py:388
  83.7 3.6 %shard_map.102 = (f32[256,512]{1,0:T(8,128)}, f32[256,512]{1,0:T(8,128)}, f32[256,512]{1,0:T(8,128)}, bf16[2048,512]{1,0:T(8,128)(2,1)}, bf16[256,512]{1,0:T(8,128)(2,1)}) custom-call(f32[256,512]{1,0:T(8,128)} %get-tuple-element.10.refs_0_, f32[256,512]{1,0:T(8,128)} %get-tuple-element.11.refs_1_, f32[256,512]{1,0:T(8,128)} %get-tuple-element.12.refs_2_, ...), custom_call_target="tpu_custom_call" | custom-call | tf_op jit(solution)/shard_map/pallas_call | solution.py:467

commit v5 on v4

--- a/solution.py
+++ b/solution.py
@@ -67,56 +67,56 @@
 
 
 SUM_ORDERS = [
-    [(3, 2, 1, 0), (2, 3, 1, 0)],
-    [(3, 2, 1, 0), (2, 3, 1, 0)],
+    [(3, 0, 1, 2), (2, 1, 3, 0)],
+    [(3, 2, 1, 0), (2, 1, 0, 3)],
 ]
 GATHER_ORDERS = [
-    [(3, 2, 1, 0), (2, 3, 1, 0)],
-    [(3, 2, 1, 0), (2, 3, 1, 0)],
+    [(2, 3, 0, 1), (3, 2, 1, 0)],
+    [(3, 0, 2, 1), (2, 1, 3, 0)],
 ]
 STEPS = [
-    ("T", 0, 15), ("T", 0, 14), ("T", 0, 13), ("T", 0, 12), ("T", 0, 11), ("S", 0, 0, 15),
-    ("S", 0, 1, 15), ("S", 0, 0, 14), ("S", 0, 1, 14), ("S", 0, 0, 13), ("S", 0, 1, 13),
-    ("S", 0, 0, 12), ("S", 0, 1, 12), ("T", 0, 7), ("S", 0, 0, 11), ("T", 0, 10), ("T", 0, 6),
-    ("T", 0, 9), ("S", 0, 1, 11), ("S", 0, 0, 7), ("S", 0, 1, 7), ("T", 0, 5), ("S", 0, 0, 10),
-    ("S", 0, 1, 10), ("S", 0, 0, 6), ("S", 0, 0, 9), ("S", 0, 1, 6), ("T", 0, 8), ("T", 0, 4),
-    ("S", 0, 1, 9), ("S", 0, 0, 5), ("S", 0, 1, 5), ("T", 0, 3), ("T", 0, 2), ("S", 0, 0, 8),
-    ("S", 0, 1, 8), ("S", 0, 0, 4), ("S", 0, 1, 4), ("T", 0, 1), ("T", 0, 0), ("T", 1, 15),
-    ("T", 1, 14), ("T", 1, 13), ("S", 0, 0, 3), ("S", 0, 1, 3), ("T", 1, 12), ("S", 1, 0, 15),
-    ("S", 1, 1, 15), ("S", 1, 0, 14), ("S", 1, 1, 14), ("S", 1, 0, 13), ("S", 1, 1, 13),
-    ("T", 1, 11), ("S", 1, 0, 12), ("S", 1, 1, 12), ("T", 1, 7), ("S", 0, 0, 2), ("T", 1, 10),
-    ("T", 1, 6), ("S", 1, 0, 11), ("S", 0, 1, 2), ("T", 1, 9), ("S", 1, 1, 11), ("T", 1, 5),
-    ("S", 1, 0, 10), ("S", 1, 1, 10), ("S", 0, 1, 1), ("S", 0, 0, 1), ("T", 1, 8), ("S", 1, 0, 9),
-    ("T", 1, 4), ("S", 1, 1, 9), ("T", 1, 3), ("T", 1, 2), ("S", 1, 0, 8), ("T", 1, 1),
-    ("S", 1, 1, 8), ("T", 1, 0), ("S", 1, 0, 7), ("S", 1, 1, 7), ("S", 1, 0, 6), ("S", 1, 1, 6),
-    ("F", 0), ("A", 0, 0, 0), ("A", 0, 1, 0), ("S", 1, 0, 5), ("S", 1, 1, 5), ("S", 1, 0, 4),
-    ("S", 1, 1, 4), ("D", 0, 0, 0), ("A", 0, 0, 1), ("D", 1, 0, 0), ("A", 0, 0, 2),
-    ("A", 0, 1, 2), ("D", 0, 0, 2), ("A", 0, 1, 1), ("D", 0, 0, 1), ("D", 1, 0, 2),
-    ("S", 1, 1, 3), ("S", 1, 0, 3), ("D", 1, 0, 1), ("S", 1, 1, 2), ("S", 1, 0, 2),
-    ("A", 0, 0, 3), ("A", 0, 0, 8), ("A", 0, 0, 4), ("A", 0, 1, 4), ("A", 0, 1, 8),
-    ("D", 0, 0, 4), ("D", 0, 0, 8), ("D", 1, 0, 8), ("S", 1, 1, 1), ("A", 0, 1, 3),
-    ("S", 1, 0, 1), ("D", 0, 0, 3), ("D", 1, 0, 4), ("D", 1, 0, 3), ("A", 0, 0, 9),
-    ("A", 0, 0, 5), ("A", 0, 0, 10), ("A", 0, 0, 6), ("A", 0, 1, 6), ("A", 0, 1, 10),
-    ("D", 0, 0, 6), ("D", 0, 0, 10), ("F", 1), ("A", 0, 1, 5), ("A", 0, 0, 7), ("A", 0, 1, 9),
-    ("A", 0, 0, 11), ("A", 1, 0, 0), ("A", 1, 1, 0), ("A", 0, 0, 12), ("A", 0, 1, 12),
-    ("D", 0, 0, 5), ("D", 1, 0, 5), ("D", 1, 0, 6), ("D", 0, 0, 9), ("D", 1, 0, 9),
-    ("D", 1, 0, 10), ("D", 0, 0, 12), ("A", 0, 1, 7), ("A", 0, 1, 11), ("D", 0, 0, 7),
-    ("D", 0, 0, 11), ("D", 1, 0, 12), ("D", 0, 1, 0), ("D", 1, 1, 0), ("A", 1, 0, 2),
-    ("A", 0, 0, 13), ("D", 1, 0, 11), ("A", 0, 1, 14), ("A", 1, 0, 1), ("D", 1, 0, 7),
-    ("A", 0, 0, 14), ("D", 0, 0, 14), ("A", 0, 1, 13), ("D", 0, 0, 13), ("A", 1, 1, 2),
-    ("D", 0, 1, 2), ("D", 1, 0, 14), ("A", 0, 0, 15), ("A", 1, 0, 4), ("A", 1, 1, 1),
-    ("D", 1, 0, 13), ("D", 0, 1, 1), ("D", 1, 1, 2), ("A", 1, 0, 8), ("A", 1, 1, 8),
-    ("D", 0, 1, 4), ("D", 1, 1, 1), ("A", 1, 0, 3), ("A", 1, 1, 4), ("A", 0, 1, 15),
-    ("D", 0, 0, 15), ("D", 1, 1, 4), ("D", 0, 1, 8), ("A", 1, 1, 3), ("D", 0, 1, 3),
-    ("D", 1, 1, 8), ("A", 1, 0, 10), ("A", 1, 0, 6), ("D", 1, 0, 15), ("D", 1, 1, 3),
-    ("A", 1, 0, 9), ("A", 1, 0, 5), ("A", 1, 1, 6), ("A", 1, 1, 10), ("D", 0, 1, 6),
-    ("D", 0, 1, 10), ("D", 1, 1, 10), ("A", 1, 0, 12), ("A", 1, 1, 9), ("D", 0, 1, 5),
-    ("D", 1, 1, 6), ("A", 1, 1, 5), ("A", 1, 0, 7), ("D", 1, 1, 5), ("D", 0, 1, 9),
-    ("D", 1, 1, 9), ("A", 1, 0, 11), ("A", 1, 1, 12), ("D", 0, 1, 12), ("A", 1, 1, 7),
-    ("A", 1, 1, 11), ("D", 0, 1, 7), ("D", 0, 1, 11), ("D", 1, 1, 12), ("D", 1, 1, 11),
-    ("A", 1, 0, 14), ("A", 1, 1, 14), ("D", 1, 1, 7), ("D", 0, 1, 14), ("A", 1, 0, 13),
-    ("A", 1, 1, 13), ("D", 0, 1, 13), ("D", 1, 1, 14), ("A", 1, 0, 15), ("D", 1, 1, 13),
-    ("A", 1, 1, 15), ("D", 0, 1, 15), ("D", 1, 1, 15),
+    ("T", 0, 15), ("T", 0, 11), ("T", 0, 14), ("T", 0, 13), ("T", 0, 7), ("S", 0, 0, 15),
+    ("S", 0, 1, 15), ("S", 0, 0, 14), ("T", 0, 9), ("S", 0, 1, 14), ("S", 0, 0, 13),
+    ("S", 0, 0, 11), ("S", 0, 1, 13), ("S", 0, 1, 11), ("T", 0, 6), ("T", 0, 10), ("S", 0, 0, 12),
+    ("S", 0, 0, 7), ("S", 0, 1, 7), ("T", 0, 12), ("T", 0, 5), ("S", 0, 1, 12), ("S", 0, 0, 10),
+    ("T", 0, 8), ("T", 0, 4), ("S", 0, 1, 10), ("S", 0, 0, 9), ("S", 0, 1, 9), ("T", 0, 3),
+    ("S", 0, 1, 6), ("S", 0, 0, 8), ("S", 0, 0, 5), ("S", 0, 1, 8), ("T", 0, 2), ("S", 0, 1, 3),
+    ("T", 0, 1), ("S", 0, 0, 6), ("S", 0, 1, 5), ("S", 0, 0, 3), ("T", 0, 0), ("T", 1, 15),
+    ("T", 1, 14), ("S", 0, 0, 4), ("T", 1, 7), ("S", 0, 1, 4), ("T", 1, 13), ("S", 0, 1, 2),
+    ("S", 1, 0, 15), ("S", 1, 1, 15), ("S", 1, 0, 14), ("S", 1, 1, 13), ("S", 1, 1, 14),
+    ("T", 1, 12), ("S", 1, 0, 13), ("S", 1, 1, 11), ("T", 1, 6), ("T", 1, 11), ("T", 1, 10),
+    ("S", 1, 0, 12), ("S", 1, 1, 9), ("T", 1, 5), ("S", 0, 1, 1), ("S", 1, 1, 12), ("S", 0, 0, 2),
+    ("S", 1, 0, 11), ("S", 1, 0, 10), ("S", 1, 1, 7), ("T", 1, 9), ("S", 0, 0, 1),
+    ("S", 1, 1, 10), ("T", 1, 8), ("S", 1, 1, 5), ("T", 1, 4), ("T", 1, 3), ("S", 1, 0, 9),
+    ("T", 1, 2), ("S", 1, 0, 8), ("S", 1, 0, 7), ("T", 1, 1), ("S", 1, 1, 8), ("S", 1, 1, 6),
+    ("T", 1, 0), ("S", 1, 0, 6), ("S", 1, 0, 5), ("S", 1, 1, 3), ("S", 1, 0, 4), ("S", 1, 1, 4),
+    ("F", 0), ("A", 0, 0, 0), ("A", 0, 1, 0), ("S", 1, 1, 2), ("D", 0, 0, 0), ("S", 1, 1, 1),
+    ("S", 1, 0, 3), ("D", 1, 0, 0), ("A", 0, 0, 4), ("S", 1, 0, 2), ("A", 0, 0, 1),
+    ("A", 0, 1, 8), ("D", 0, 0, 8), ("D", 1, 0, 8), ("A", 0, 0, 5), ("A", 0, 0, 8),
+    ("A", 0, 1, 2), ("A", 0, 0, 2), ("A", 0, 1, 4), ("D", 0, 0, 2), ("D", 0, 0, 4),
+    ("D", 1, 0, 2), ("A", 0, 1, 1), ("A", 0, 0, 12), ("D", 0, 0, 1), ("D", 1, 0, 4),
+    ("A", 0, 0, 9), ("A", 0, 1, 10), ("S", 1, 0, 1), ("D", 0, 0, 10), ("D", 1, 0, 1),
+    ("D", 1, 0, 10), ("A", 0, 0, 3), ("A", 0, 0, 6), ("A", 0, 0, 13), ("A", 0, 1, 12),
+    ("D", 0, 0, 12), ("A", 0, 1, 6), ("A", 0, 1, 9), ("A", 0, 1, 3), ("F", 1), ("A", 0, 1, 5),
+    ("A", 0, 0, 7), ("A", 0, 0, 10), ("A", 1, 0, 0), ("A", 0, 1, 14), ("A", 1, 1, 0),
+    ("D", 0, 0, 3), ("A", 0, 0, 11), ("D", 1, 0, 3), ("D", 0, 0, 5), ("D", 1, 0, 5),
+    ("D", 0, 0, 6), ("A", 0, 1, 11), ("D", 1, 0, 6), ("D", 0, 0, 9), ("D", 1, 0, 9),
+    ("A", 0, 0, 14), ("D", 0, 0, 11), ("D", 1, 0, 12), ("A", 1, 0, 1), ("A", 0, 1, 7),
+    ("D", 0, 0, 7), ("D", 1, 0, 11), ("D", 0, 0, 14), ("D", 1, 0, 14), ("A", 0, 1, 13),
+    ("D", 0, 0, 13), ("D", 0, 1, 0), ("D", 1, 1, 0), ("D", 1, 0, 7), ("D", 1, 0, 13),
+    ("A", 1, 0, 8), ("A", 0, 0, 15), ("A", 1, 1, 2), ("D", 0, 1, 8), ("A", 1, 0, 2),
+    ("A", 1, 1, 4), ("D", 0, 1, 2), ("A", 1, 0, 4), ("D", 1, 1, 8), ("A", 1, 1, 8),
+    ("D", 0, 1, 4), ("A", 1, 0, 9), ("D", 1, 1, 2), ("A", 1, 1, 1), ("A", 0, 1, 15),
+    ("A", 1, 0, 3), ("D", 0, 0, 15), ("D", 0, 1, 1), ("D", 1, 1, 4), ("A", 1, 1, 6),
+    ("D", 0, 1, 10), ("D", 1, 1, 1), ("D", 1, 0, 15), ("A", 1, 0, 5), ("A", 1, 1, 10),
+    ("A", 1, 0, 10), ("D", 0, 1, 12), ("D", 1, 1, 10), ("A", 1, 1, 12), ("D", 0, 1, 6),
+    ("A", 1, 0, 12), ("D", 1, 1, 12), ("A", 1, 1, 5), ("D", 0, 1, 3), ("D", 1, 1, 6),
+    ("A", 1, 1, 9), ("A", 1, 1, 3), ("D", 1, 1, 3), ("A", 1, 0, 6), ("A", 1, 1, 14),
+    ("D", 0, 1, 5), ("D", 0, 1, 9), ("A", 1, 0, 11), ("D", 1, 1, 9), ("A", 1, 1, 7),
+    ("A", 1, 0, 7), ("A", 1, 1, 13), ("D", 1, 1, 5), ("A", 1, 0, 13), ("D", 0, 1, 7),
+    ("D", 0, 1, 11), ("D", 0, 1, 14), ("D", 1, 1, 14), ("D", 1, 1, 7), ("A", 1, 1, 11),
+    ("A", 1, 0, 14), ("D", 1, 1, 11), ("D", 0, 1, 13), ("A", 1, 1, 15), ("A", 1, 0, 15),
+    ("D", 1, 1, 13), ("D", 0, 1, 15), ("D", 1, 1, 15),
 ]
 
 

time: 87.5 us -> 84.1 us (0.961)
  Pallas kernels: 86.6 us -> 83.1 us
    pallas_call x1, Pallas kernels: 83.1 us -> 79.5 us  [local_kernel(): pl.pallas_call(functools.partial(kernel, plan), out_shape=(jax.ShapeDtype...]
where the time goes in v5:
time: 84.1 us; the launch traced here: 83.7 us
  Pallas kernels  83.1 us (99%)
    pallas_call x1, Pallas kernels, local_kernel(): pl.pallas_call(functools.partial(kernel, plan), out_shape=(jax.ShapeDtype...  79.5 us
    pallas_call x1, Pallas kernels, hand_on(): pl.pallas_call(functools.partial(copy_kernel, pieces), out_shape=tuple((j...  3.58 us

profile of v5, /device:TPU:1, one launch (start us, length us, event | category | flops | bytes accessed | tf_op | source)
XLA Modules:
  0.0 83.7 jit_solution(16678919711290914606)
XLA Ops:
  0.6 79.5 %shard_map.101 = (f32[256,512]{1,0:T(8,128)}, f32[256,512]{1,0:T(8,128)}, f32[256,512]{1,0:T(8,128)}, bf16[2048,512]{1,0:T(8,128)(2,1)}, bf16[256,512]{1,0:T(8,128)(2,1)}) custom-call(bf16[256,8192]{1,0:T(8,128)(2,1)} %refs_0_.1, bf16[256,512]{1,0:T(8,128)(2,1)} %refs_1_.1, f32[256,512]{1,0:T(8,128)} %refs_2_.1, f32[256,512]{1,0:T(8,128)} %refs_3_.1, ...), custom_call_target="tpu_custom_call" | custom-call | flops 4294967296 | bytes 11534336 | tf_op jit(solution)/shard_map/pallas_call | solution.py:388
  80.1 3.6 %shard_map.102 = (f32[256,512]{1,0:T(8,128)}, f32[256,512]{1,0:T(8,128)}, f32[256,512]{1,0:T(8,128)}, bf16[2048,512]{1,0:T(8,128)(2,1)}, bf16[256,512]{1,0:T(8,128)(2,1)}) custom-call(f32[256,512]{1,0:T(8,128)} %get-tuple-element.10.refs_0_, f32[256,512]{1,0:T(8,128)} %get-tuple-element.11.refs_1_, f32[256,512]{1,0:T(8,128)} %get-tuple-element.12.refs_2_, ...), custom_call_target="tpu_custom_call" | custom-call | tf_op jit(solution)/shard_map/pallas_call | solution.py:467

commit v6 on v5

--- a/solution.py
+++ b/solution.py
@@ -221,7 +221,7 @@
     grad_t[...] = grad[...].astype(F32).T.astype(BF16)
     pl.semaphore_wait(barrier, 1 + depth)
 
-    cores, sums, passed, crossed, stores = {}, {}, {}, {}, []
+    cores, sums, passed, crossed, met, stores = {}, {}, {}, {}, {}, []
     done = set()
 
     def once(key, wait):
@@ -244,7 +244,7 @@
         copy = pltpu.make_async_remote_copy(
             src_ref=snd0.at[at],
             dst_ref=rcv0.at[at],
-            send_sem=core_send.at[g, c],
+            send_sem=core_send.at[0],
             recv_sem=core_recv.at[g, c],
             device_id=sibling,
             device_id_type=MESH,
@@ -279,7 +279,7 @@
         copy = pltpu.make_async_remote_copy(
             src_ref=own.at[plan.canon(order, k), pl.ds(g * wide + p * count, count)],
             dst_ref=rv[(g, p)][step].at[k - 2**high],
-            send_sem=rs_send.at[g * parts + p, k],
+            send_sem=rs_send.at[0],
             recv_sem=rs_recv.at[g * parts + p, k],
             device_id=others[order[step]],
             device_id_type=MESH,
@@ -315,31 +315,32 @@
             copy = pltpu.make_async_remote_copy(
                 src_ref=weights.at[0, g, c, rows],
                 dst_ref=weights.at[0, g, c + 2**e, rows],
-                send_sem=ag_send.at[g * parts + p, q + 2**t],
+                send_sem=ag_send.at[0],
                 recv_sem=ag_recv.at[g * parts + p, q + 2**t],
                 device_id=others[e],
                 device_id_type=MESH,
             )
             copy.start()
             passed[(g, p, q + 2**t)] = copy
-        copy = pltpu.make_async_remote_copy(
-            src_ref=weights.at[0, g, c, rows],
-            dst_ref=weights.at[1, g, c, rows],
-            send_sem=cg_send.at[g * parts + p, c],
-            recv_sem=cg_recv.at[g * parts + p, c],
-            device_id=sibling,
-            device_id_type=MESH,
-        )
-        copy.start()
-        crossed[(g, p, c)] = copy
+        met[(g, c)] = met.get((g, c), 0) + 1
+        if met[(g, c)] == parts:
+            copy = pltpu.make_async_remote_copy(
+                src_ref=weights.at[0, g, c],
+                dst_ref=weights.at[1, g, c],
+                send_sem=cg_send.at[0],
+                recv_sem=cg_recv.at[g, c],
+                device_id=sibling,
+                device_id_type=MESH,
+            )
+            copy.start()
+            crossed[(g, c)] = copy
 
     inner_mask = sum(2**j for j, (axis, _) in enumerate(plan.dims) if axis == "inner")
 
     def project(side, g, c):
         span = group_span(g)
         if side == 1:
-            for p in range(parts):
-                crossed[(g, p, c)].wait_recv()
+            crossed[(g, c)].wait_recv()
         elif c & inner_mask == 0:
             o, _ = block_at(False, c)
             keep = pltpu.make_async_copy(
@@ -364,9 +365,14 @@
         run[step[0]](*step[1:])
     proj_o[...] = acc[...].astype(BF16)
 
-    for group in (cores, sums, passed, crossed):
-        for copy in group.values():
-            copy.wait_send()
+    sent = [
+        (core_send, rcv0),
+        (rs_send, own.at[pl.ds(1, blocks - 1)]),
+        (ag_send, weights.at[0, :, pl.ds(1, blocks - 1)]),
+        (cg_send, weights.at[0]),
+    ]
+    for sem, ref in sent:
+        pltpu.make_async_copy(ref, ref, sem.at[0]).wait()
     for copy in stores:
         copy.wait()
 
@@ -414,14 +420,14 @@
         + arrived
         + [
             dma((2, B)),
+            dma((1,)),
             dma((G, B)),
+            dma((1,)),
+            dma((n_parts, B)),
+            dma((1,)),
+            dma((n_parts, B)),
+            dma((1,)),
             dma((G, B)),
-            dma((n_parts, B)),
-            dma((n_parts, B)),
-            dma((n_parts, B)),
-            dma((n_parts, B)),
-            dma((n_parts, B)),
-            dma((n_parts, B)),
             dma((5,)),
             dma((G, 3 + B)),
         ],
@@ -462,7 +468,7 @@
         copy.wait()
 
 
-def hand_on(arrays, pieces=2):
+def hand_on(arrays, pieces=4):
     any_spec = pl.BlockSpec(memory_space=pl.ANY)
     return pl.pallas_call(
         functools.partial(copy_kernel, pieces),

time: 84.1 us -> 81.9 us (0.974)
  Pallas kernels: 83.1 us -> 80.9 us
    pallas_call x1, Pallas kernels: 79.5 us -> 76.9 us  [local_kernel(): pl.pallas_call(functools.partial(kernel, plan), out_shape=(jax.ShapeDtype...]
where the time goes in v6:
time: 81.9 us; the launch traced here: 81.5 us
  Pallas kernels  80.9 us (99%)
    pallas_call x1, Pallas kernels, local_kernel(): pl.pallas_call(functools.partial(kernel, plan), out_shape=(jax.ShapeDtype...  76.9 us
    pallas_call x1, Pallas kernels, hand_on(): pl.pallas_call(functools.partial(copy_kernel, pieces), out_shape=tuple((j...  4 us

profile of v6, /device:TPU:1, one launch (start us, length us, event | category | flops | bytes accessed | tf_op | source)
XLA Modules:
  0.0 81.5 jit_solution(2047237925185085368)
XLA Ops:
  0.6 76.9 %shard_map.101 = (f32[256,512]{1,0:T(8,128)}, f32[256,512]{1,0:T(8,128)}, f32[256,512]{1,0:T(8,128)}, bf16[2048,512]{1,0:T(8,128)(2,1)}, bf16[256,512]{1,0:T(8,128)(2,1)}) custom-call(bf16[256,8192]{1,0:T(8,128)(2,1)} %refs_0_.1, bf16[256,512]{1,0:T(8,128)(2,1)} %refs_1_.1, f32[256,512]{1,0:T(8,128)} %refs_2_.1, f32[256,512]{1,0:T(8,128)} %refs_3_.1, ...), custom_call_target="tpu_custom_call" | custom-call | flops 4294967296 | bytes 11534336 | tf_op jit(solution)/shard_map/pallas_call | solution.py:394
  77.5 4.0 %shard_map.102 = (f32[256,512]{1,0:T(8,128)}, f32[256,512]{1,0:T(8,128)}, f32[256,512]{1,0:T(8,128)}, bf16[2048,512]{1,0:T(8,128)(2,1)}, bf16[256,512]{1,0:T(8,128)(2,1)}) custom-call(f32[256,512]{1,0:T(8,128)} %get-tuple-element.10.refs_0_, f32[256,512]{1,0:T(8,128)} %get-tuple-element.11.refs_1_, f32[256,512]{1,0:T(8,128)} %get-tuple-element.12.refs_2_, ...), custom_call_target="tpu_custom_call" | custom-call | tf_op jit(solution)/shard_map/pallas_call | solution.py:473

commit v7 on v6

--- a/solution.py
+++ b/solution.py
@@ -67,56 +67,56 @@
 
 
 SUM_ORDERS = [
-    [(3, 0, 1, 2), (2, 1, 3, 0)],
-    [(3, 2, 1, 0), (2, 1, 0, 3)],
+    [(3, 0, 2, 1), (2, 1, 3, 0)],
+    [(3, 2, 1, 0), (2, 3, 0, 1)],
 ]
 GATHER_ORDERS = [
     [(2, 3, 0, 1), (3, 2, 1, 0)],
-    [(3, 0, 2, 1), (2, 1, 3, 0)],
+    [(3, 1, 2, 0), (2, 1, 3, 0)],
 ]
 STEPS = [
-    ("T", 0, 15), ("T", 0, 11), ("T", 0, 14), ("T", 0, 13), ("T", 0, 7), ("S", 0, 0, 15),
-    ("S", 0, 1, 15), ("S", 0, 0, 14), ("T", 0, 9), ("S", 0, 1, 14), ("S", 0, 0, 13),
-    ("S", 0, 0, 11), ("S", 0, 1, 13), ("S", 0, 1, 11), ("T", 0, 6), ("T", 0, 10), ("S", 0, 0, 12),
-    ("S", 0, 0, 7), ("S", 0, 1, 7), ("T", 0, 12), ("T", 0, 5), ("S", 0, 1, 12), ("S", 0, 0, 10),
-    ("T", 0, 8), ("T", 0, 4), ("S", 0, 1, 10), ("S", 0, 0, 9), ("S", 0, 1, 9), ("T", 0, 3),
-    ("S", 0, 1, 6), ("S", 0, 0, 8), ("S", 0, 0, 5), ("S", 0, 1, 8), ("T", 0, 2), ("S", 0, 1, 3),
-    ("T", 0, 1), ("S", 0, 0, 6), ("S", 0, 1, 5), ("S", 0, 0, 3), ("T", 0, 0), ("T", 1, 15),
-    ("T", 1, 14), ("S", 0, 0, 4), ("T", 1, 7), ("S", 0, 1, 4), ("T", 1, 13), ("S", 0, 1, 2),
-    ("S", 1, 0, 15), ("S", 1, 1, 15), ("S", 1, 0, 14), ("S", 1, 1, 13), ("S", 1, 1, 14),
-    ("T", 1, 12), ("S", 1, 0, 13), ("S", 1, 1, 11), ("T", 1, 6), ("T", 1, 11), ("T", 1, 10),
-    ("S", 1, 0, 12), ("S", 1, 1, 9), ("T", 1, 5), ("S", 0, 1, 1), ("S", 1, 1, 12), ("S", 0, 0, 2),
-    ("S", 1, 0, 11), ("S", 1, 0, 10), ("S", 1, 1, 7), ("T", 1, 9), ("S", 0, 0, 1),
-    ("S", 1, 1, 10), ("T", 1, 8), ("S", 1, 1, 5), ("T", 1, 4), ("T", 1, 3), ("S", 1, 0, 9),
-    ("T", 1, 2), ("S", 1, 0, 8), ("S", 1, 0, 7), ("T", 1, 1), ("S", 1, 1, 8), ("S", 1, 1, 6),
-    ("T", 1, 0), ("S", 1, 0, 6), ("S", 1, 0, 5), ("S", 1, 1, 3), ("S", 1, 0, 4), ("S", 1, 1, 4),
-    ("F", 0), ("A", 0, 0, 0), ("A", 0, 1, 0), ("S", 1, 1, 2), ("D", 0, 0, 0), ("S", 1, 1, 1),
-    ("S", 1, 0, 3), ("D", 1, 0, 0), ("A", 0, 0, 4), ("S", 1, 0, 2), ("A", 0, 0, 1),
-    ("A", 0, 1, 8), ("D", 0, 0, 8), ("D", 1, 0, 8), ("A", 0, 0, 5), ("A", 0, 0, 8),
-    ("A", 0, 1, 2), ("A", 0, 0, 2), ("A", 0, 1, 4), ("D", 0, 0, 2), ("D", 0, 0, 4),
-    ("D", 1, 0, 2), ("A", 0, 1, 1), ("A", 0, 0, 12), ("D", 0, 0, 1), ("D", 1, 0, 4),
-    ("A", 0, 0, 9), ("A", 0, 1, 10), ("S", 1, 0, 1), ("D", 0, 0, 10), ("D", 1, 0, 1),
-    ("D", 1, 0, 10), ("A", 0, 0, 3), ("A", 0, 0, 6), ("A", 0, 0, 13), ("A", 0, 1, 12),
-    ("D", 0, 0, 12), ("A", 0, 1, 6), ("A", 0, 1, 9), ("A", 0, 1, 3), ("F", 1), ("A", 0, 1, 5),
-    ("A", 0, 0, 7), ("A", 0, 0, 10), ("A", 1, 0, 0), ("A", 0, 1, 14), ("A", 1, 1, 0),
-    ("D", 0, 0, 3), ("A", 0, 0, 11), ("D", 1, 0, 3), ("D", 0, 0, 5), ("D", 1, 0, 5),
-    ("D", 0, 0, 6), ("A", 0, 1, 11), ("D", 1, 0, 6), ("D", 0, 0, 9), ("D", 1, 0, 9),
-    ("A", 0, 0, 14), ("D", 0, 0, 11), ("D", 1, 0, 12), ("A", 1, 0, 1), ("A", 0, 1, 7),
-    ("D", 0, 0, 7), ("D", 1, 0, 11), ("D", 0, 0, 14), ("D", 1, 0, 14), ("A", 0, 1, 13),
-    ("D", 0, 0, 13), ("D", 0, 1, 0), ("D", 1, 1, 0), ("D", 1, 0, 7), ("D", 1, 0, 13),
-    ("A", 1, 0, 8), ("A", 0, 0, 15), ("A", 1, 1, 2), ("D", 0, 1, 8), ("A", 1, 0, 2),
-    ("A", 1, 1, 4), ("D", 0, 1, 2), ("A", 1, 0, 4), ("D", 1, 1, 8), ("A", 1, 1, 8),
-    ("D", 0, 1, 4), ("A", 1, 0, 9), ("D", 1, 1, 2), ("A", 1, 1, 1), ("A", 0, 1, 15),
-    ("A", 1, 0, 3), ("D", 0, 0, 15), ("D", 0, 1, 1), ("D", 1, 1, 4), ("A", 1, 1, 6),
-    ("D", 0, 1, 10), ("D", 1, 1, 1), ("D", 1, 0, 15), ("A", 1, 0, 5), ("A", 1, 1, 10),
-    ("A", 1, 0, 10), ("D", 0, 1, 12), ("D", 1, 1, 10), ("A", 1, 1, 12), ("D", 0, 1, 6),
-    ("A", 1, 0, 12), ("D", 1, 1, 12), ("A", 1, 1, 5), ("D", 0, 1, 3), ("D", 1, 1, 6),
-    ("A", 1, 1, 9), ("A", 1, 1, 3), ("D", 1, 1, 3), ("A", 1, 0, 6), ("A", 1, 1, 14),
-    ("D", 0, 1, 5), ("D", 0, 1, 9), ("A", 1, 0, 11), ("D", 1, 1, 9), ("A", 1, 1, 7),
-    ("A", 1, 0, 7), ("A", 1, 1, 13), ("D", 1, 1, 5), ("A", 1, 0, 13), ("D", 0, 1, 7),
-    ("D", 0, 1, 11), ("D", 0, 1, 14), ("D", 1, 1, 14), ("D", 1, 1, 7), ("A", 1, 1, 11),
-    ("A", 1, 0, 14), ("D", 1, 1, 11), ("D", 0, 1, 13), ("A", 1, 1, 15), ("A", 1, 0, 15),
-    ("D", 1, 1, 13), ("D", 0, 1, 15), ("D", 1, 1, 15),
+    ("T", 0, 15), ("T", 0, 13), ("T", 0, 14), ("T", 0, 11), ("T", 0, 7), ("S", 0, 0, 15),
+    ("S", 0, 1, 15), ("S", 0, 0, 14), ("S", 0, 1, 14), ("S", 0, 0, 11), ("S", 0, 0, 13),
+    ("S", 0, 1, 11), ("S", 0, 1, 13), ("T", 0, 9), ("T", 0, 6), ("S", 0, 0, 7), ("S", 0, 1, 7),
+    ("T", 0, 12), ("T", 0, 10), ("S", 0, 0, 12), ("S", 0, 1, 12), ("T", 0, 5), ("T", 0, 8),
+    ("S", 0, 0, 10), ("S", 0, 1, 10), ("S", 0, 0, 9), ("S", 0, 1, 6), ("T", 0, 4), ("S", 0, 1, 9),
+    ("S", 0, 0, 8), ("S", 0, 0, 6), ("S", 0, 0, 3), ("S", 0, 1, 3), ("T", 0, 3), ("S", 0, 1, 8),
+    ("T", 0, 2), ("T", 0, 1), ("S", 0, 1, 2), ("T", 0, 0), ("S", 0, 0, 5), ("S", 0, 1, 5),
+    ("S", 0, 1, 4), ("T", 1, 15), ("S", 0, 0, 4), ("S", 0, 0, 2), ("T", 1, 14), ("T", 1, 13),
+    ("T", 1, 12), ("S", 1, 0, 15), ("S", 1, 1, 15), ("T", 1, 11), ("S", 1, 0, 14),
+    ("S", 1, 1, 14), ("S", 1, 0, 13), ("S", 1, 1, 13), ("S", 0, 0, 1), ("S", 1, 0, 12),
+    ("S", 0, 1, 1), ("S", 1, 1, 12), ("S", 1, 0, 11), ("S", 1, 1, 7), ("T", 1, 7), ("T", 1, 10),
+    ("T", 1, 5), ("T", 1, 9), ("T", 1, 6), ("S", 1, 1, 11), ("S", 1, 0, 10), ("S", 1, 0, 7),
+    ("S", 1, 1, 10), ("S", 1, 0, 5), ("S", 1, 0, 9), ("F", 0), ("A", 0, 0, 0), ("A", 0, 1, 0),
+    ("S", 1, 1, 9), ("S", 1, 0, 6), ("S", 1, 1, 6), ("S", 1, 1, 5), ("T", 1, 8), ("T", 1, 4),
+    ("A", 0, 0, 1), ("T", 1, 3), ("T", 1, 2), ("A", 0, 0, 4), ("S", 1, 0, 8), ("S", 1, 1, 8),
+    ("S", 1, 0, 4), ("S", 1, 1, 4), ("S", 1, 0, 3), ("A", 0, 1, 8), ("S", 1, 1, 3),
+    ("A", 0, 0, 8), ("T", 1, 1), ("A", 0, 1, 2), ("A", 0, 0, 2), ("A", 0, 1, 4), ("T", 1, 0),
+    ("D", 0, 0, 0), ("A", 0, 1, 1), ("S", 1, 0, 2), ("S", 1, 1, 2), ("D", 1, 0, 0),
+    ("D", 0, 0, 1), ("S", 1, 0, 1), ("D", 0, 0, 2), ("A", 0, 0, 3), ("A", 0, 0, 5),
+    ("D", 1, 0, 1), ("D", 1, 0, 2), ("A", 0, 0, 9), ("D", 0, 0, 4), ("A", 0, 1, 3),
+    ("D", 0, 0, 3), ("S", 1, 1, 1), ("D", 1, 0, 4), ("A", 0, 0, 12), ("D", 0, 0, 8),
+    ("D", 1, 0, 8), ("D", 1, 0, 3), ("A", 0, 1, 10), ("D", 0, 0, 10), ("A", 0, 0, 6),
+    ("A", 0, 1, 6), ("D", 0, 0, 6), ("D", 1, 0, 10), ("A", 0, 1, 12), ("D", 0, 0, 12), ("F", 1),
+    ("A", 0, 1, 5), ("A", 0, 0, 7), ("A", 0, 1, 9), ("A", 0, 0, 10), ("A", 0, 0, 11),
+    ("A", 0, 1, 11), ("A", 0, 0, 13), ("A", 0, 1, 14), ("A", 1, 0, 0), ("A", 1, 1, 0),
+    ("A", 0, 1, 7), ("D", 0, 0, 5), ("A", 0, 1, 13), ("A", 0, 0, 14), ("D", 1, 0, 5),
+    ("D", 1, 0, 6), ("D", 0, 0, 7), ("D", 0, 0, 9), ("A", 0, 0, 15), ("D", 1, 0, 7),
+    ("A", 1, 0, 8), ("D", 1, 0, 9), ("D", 0, 0, 11), ("D", 1, 0, 11), ("D", 1, 0, 12),
+    ("D", 0, 0, 13), ("D", 1, 0, 13), ("A", 1, 0, 2), ("A", 1, 1, 2), ("A", 1, 1, 8),
+    ("D", 0, 0, 14), ("A", 0, 1, 15), ("A", 1, 0, 1), ("A", 1, 0, 4), ("D", 1, 0, 14),
+    ("D", 0, 0, 15), ("D", 0, 1, 0), ("A", 1, 1, 1), ("A", 1, 1, 4), ("A", 1, 0, 10),
+    ("A", 1, 1, 10), ("D", 1, 0, 15), ("A", 1, 0, 6), ("D", 1, 1, 0), ("A", 1, 0, 9),
+    ("D", 0, 1, 1), ("A", 1, 0, 3), ("D", 1, 1, 1), ("D", 0, 1, 2), ("D", 1, 1, 2),
+    ("A", 1, 0, 12), ("A", 1, 1, 6), ("A", 1, 1, 9), ("D", 0, 1, 4), ("D", 1, 1, 4),
+    ("D", 0, 1, 5), ("D", 0, 1, 8), ("A", 1, 0, 5), ("A", 1, 1, 12), ("A", 1, 1, 3),
+    ("A", 1, 1, 5), ("A", 1, 0, 14), ("D", 0, 1, 3), ("D", 1, 1, 5), ("A", 1, 1, 14),
+    ("D", 0, 1, 6), ("A", 1, 0, 7), ("D", 1, 1, 6), ("A", 1, 0, 11), ("D", 1, 1, 3),
+    ("D", 1, 1, 8), ("D", 0, 1, 9), ("A", 1, 1, 7), ("A", 1, 1, 11), ("A", 1, 0, 13),
+    ("D", 1, 1, 9), ("D", 0, 1, 10), ("D", 1, 1, 10), ("D", 0, 1, 11), ("A", 1, 1, 13),
+    ("D", 0, 1, 7), ("A", 1, 0, 15), ("D", 1, 1, 11), ("D", 0, 1, 12), ("D", 1, 1, 12),
+    ("D", 0, 1, 13), ("A", 1, 1, 15), ("D", 1, 1, 7), ("D", 1, 1, 13), ("D", 0, 1, 14),
+    ("D", 1, 1, 14), ("D", 0, 1, 15), ("D", 1, 1, 15),
 ]
 
 
@@ -468,7 +468,7 @@
         copy.wait()
 
 
-def hand_on(arrays, pieces=4):
+def hand_on(arrays, pieces=2):
     any_spec = pl.BlockSpec(memory_space=pl.ANY)
     return pl.pallas_call(
         functools.partial(copy_kernel, pieces),

time: 81.9 us -> 82.2 us (level)
    pallas_call x1, Pallas kernels: 76.9 us -> 77.8 us  [local_kernel(): pl.pallas_call(functools.partial(kernel, plan), out_shape=(jax.ShapeDtype...]
where the time goes in v7:
time: 82.2 us; the launch traced here: 82 us
  Pallas kernels  81.4 us (99%)
    pallas_call x1, Pallas kernels, local_kernel(): pl.pallas_call(functools.partial(kernel, plan), out_shape=(jax.ShapeDtype...  77.8 us
    pallas_call x1, Pallas kernels, hand_on(): pl.pallas_call(functools.partial(copy_kernel, pieces), out_shape=tuple((j...  3.58 us

profile of v7, /device:TPU:1, one launch (start us, length us, event | category | flops | bytes accessed | tf_op | source)
XLA Modules:
  0.0 82.0 jit_solution(16806559164285023769)
XLA Ops:
  0.6 77.8 %shard_map.101 = (f32[256,512]{1,0:T(8,128)}, f32[256,512]{1,0:T(8,128)}, f32[256,512]{1,0:T(8,128)}, bf16[2048,512]{1,0:T(8,128)(2,1)}, bf16[256,512]{1,0:T(8,128)(2,1)}) custom-call(bf16[256,8192]{1,0:T(8,128)(2,1)} %refs_0_.1, bf16[256,512]{1,0:T(8,128)(2,1)} %refs_1_.1, f32[256,512]{1,0:T(8,128)} %refs_2_.1, f32[256,512]{1,0:T(8,128)} %refs_3_.1, ...), custom_call_target="tpu_custom_call" | custom-call | flops 4294967296 | bytes 11534336 | tf_op jit(solution)/shard_map/pallas_call | solution.py:394
  78.4 3.6 %shard_map.102 = (f32[256,512]{1,0:T(8,128)}, f32[256,512]{1,0:T(8,128)}, f32[256,512]{1,0:T(8,128)}, bf16[2048,512]{1,0:T(8,128)(2,1)}, bf16[256,512]{1,0:T(8,128)(2,1)}) custom-call(f32[256,512]{1,0:T(8,128)} %get-tuple-element.10.refs_0_, f32[256,512]{1,0:T(8,128)} %get-tuple-element.11.refs_1_, f32[256,512]{1,0:T(8,128)} %get-tuple-element.12.refs_2_, ...), custom_call_target="tpu_custom_call" | custom-call | tf_op jit(solution)/shard_map/pallas_call | solution.py:473
